TPU v7x, 128 devices: a whole 4x4x4 slice. The times are simulated.
128 devices in a mesh: rep: 8 (over y, x_hi), fsdp: 16 (over z, x_lo, core).
Axes of the slice: x: 4 (x_hi: 2, x_lo: 2; x = x_hi * 2 + x_lo), y: 4, z: 4, core: 2. Of those that a mesh axis runs over, the one named last changes fastest.
Arguments:
- step_bit: int32 [], replicated, may hold values from 0 to 999
- tokens: bfloat16 [8, 16384, 5120], P('rep', 'fsdp'), may hold values from -6 to 6
- target: bfloat16 [8, 16384, 1024], P('rep', 'fsdp'), may hold values from -6 to 6
- norm_gain: float32 [5120], replicated, may hold values from 0.5 to 2
- weights: bfloat16 [8, 5120, 1024], P('rep', 'fsdp')
- previous: bfloat16 [8, 5120, 1024], P('rep', 'fsdp')
- anchor: float32 [8, 5120, 1024], P('rep', 'fsdp')
- momentum: float32 [8, 5120, 1024], P('rep', 'fsdp'), may hold values from -6 to 6
Outputs:
- new_momentum: float32 [8, 5120, 1024], P('rep', 'fsdp')
- new_anchor: float32 [8, 5120, 1024], P('rep', 'fsdp')
All inputs are finite; a program needn't handle non-finite values.
Results may differ from a plain program's by a relative error of at most 0.0022.
Values may be sent and summed in bfloat16 or wider, within the bound.
A program may use at most 192 MiB of HBM per device.

v0:
```python
import jax
import jax.numpy as jnp
from jax import lax
from jax.sharding import PartitionSpec as P

EPS = 1e-06
INNER_RATE = 0.05
OUTER_RATE = 1.0
SLOW_BETA = 0.6


def swapped(value, axis, apart):
    mask = 2**apart
    pairs = [(source, source ^ mask) for source in range(lax.axis_size(axis))]
    return lax.ppermute(value, axis, pairs)


def shards(step_bit, tokens, target, norm_gain, weights, previous, anchor, momentum):
    token_rows = tokens[0].astype(jnp.float32)
    scale_rms = lax.rsqrt(jnp.mean(token_rows * token_rows, axis=-1, keepdims=True) + EPS)
    normed = (token_rows * scale_rms * norm_gain).astype(jnp.bfloat16)
    model_width = normed.shape[1]
    columns = normed
    values = jnp.dot(
        columns,
        lax.all_gather(weights[0], "fsdp", axis=0, tiled=True),
        preferred_element_type=jnp.float32,
    ) * model_width ** (-0.5)
    error = (values - target[0].astype(jnp.float32)).astype(jnp.bfloat16)
    columns = normed
    gradient = lax.psum_scatter(
        lax.dot_general(
            columns, error, (((0,), (0,)), ((), ())), preferred_element_type=jnp.float32
        ),
        "fsdp",
        scatter_dimension=0,
        tiled=True,
    )
    gradient = gradient * model_width ** (-0.5)
    bit_count = lax.axis_size("rep").bit_length() - 1
    chosen_bit = jnp.remainder(step_bit, jnp.int32(bit_count))
    received = jnp.zeros_like(previous[0])
    for bit_value in range(bit_count):
        arrived = swapped(previous[0], "rep", bit_value)
        received = jnp.where(chosen_bit == bit_value, arrived, received)
    fast_weights = weights[0].astype(jnp.float32) - INNER_RATE * gradient
    mixed = 0.5 * fast_weights + 0.5 * received.astype(jnp.float32)
    moment_new = SLOW_BETA * momentum[0] + (anchor[0] - mixed) / INNER_RATE
    anchor_new = anchor[0] - OUTER_RATE * INNER_RATE * moment_new
    return (moment_new[None], anchor_new[None])


def solution(mesh):
    placed = (
        P(),
        P("rep", "fsdp", None),
        P("rep", "fsdp", None),
        P(),
        P("rep", "fsdp", None),
        P("rep", "fsdp", None),
        P("rep", "fsdp", None),
        P("rep", "fsdp", None),
    )
    return jax.shard_map(
        shards,
        mesh=mesh,
        in_specs=placed,
        out_specs=(P("rep", "fsdp", None), P("rep", "fsdp", None)),
        check_vma=False,
    )
```

profile of v0, /device:TPU:1, one launch (start us, length us, event | category | flops | bytes accessed | tf_op | source)
XLA Modules:
  0.0 353.6 jit_solution(322073413319754378)
XLA Ops:
  7.2 0.0 all-gather.3.cloned.1.call-start
  7.2 0.7 all-gather.3.cloned.1.call-update
  7.9 0.0 copy-start.4
  7.9 0.0 reduce-scatter.2.cloned.1.call-start
  8.0 6.1 %fusion = f32[1024]{0:T(1024)S(1)} fusion(bf16[1,1024,5120]{2,1,0:T(8,128)(2,1)} %param.9), kind=kLoop, calls=%fused_computation.2 | loop fusion | flops 15727616 | bytes 10489856 | tf_op jit(solution)/shard_map/reduce_sum | solution.py:20
  14.0 0.0 copy-start.3
  14.1 61.3 %all-gather.3.cloned.1.call-done = bf16[1,5120,1024]{2,1,0:T(8,128)(2,1)} async-done(((bf16[1,320,1024]{2,1,0:T(8,128)(2,1)}), bf16[1,5120,1024]{2,1,0:T(8,128)(2,1)}) %all-gather.3.cloned.1.call-update) | async-done | bytes 10485776 | tf_op jit(solution)/shard_map/all_gather | solution.py:26
  75.4 0.0 copy-done.4
  75.4 15.5 %fusion.3 = f32[1024,1024]{1,0:T(8,128)S(1)} fusion(bf16[1,5120,1024]{2,1,0:T(8,128)(2,1)} %all-gather.3.cloned.1.call-done, bf16[1,1024,5120]{2,1,0:T(8,128)(2,1)} %param.9, f32[5120]{0:T(1024)S(1)} %copy-done.4, f32[1024]{0:T(1024)S(1)} %add_rsqrt_fusion), kind=kOutput, calls=%fused_computation.5 | convolution fusion | flops 10758389760 | bytes 25190400 | tf_op jit(solution)/shard_map/dot_general | solution.py:24
  90.9 0.0 copy-done.3
  90.9 18.3 %fusion.6 = f32[5120,1024]{1,0:T(8,128)} fusion(bf16[1,1024,5120]{2,1,0:T(8,128)(2,1)} %param.9, f32[5120]{0:T(1024)S(1)} %copy-done.4, f32[1024]{0:T(1024)S(1)} %add_rsqrt_fusion, f32[1024,1024]{1,0:T(8,128)S(1)} %fusion.3, bf16[1,1024,1024]{2,1,0:T(8,128)(2,1)S(1)} %copy-done.3), kind=kOutput, calls=%fused_computation.9 | convolution fusion | flops 10762584064 | bytes 37773312 | tf_op jit(solution)/shard_map/dot_general | solution.py:32
  109.2 0.0 copy-start
  109.3 0.0 copy-start.1
  109.3 0.0 copy-start.2
  109.3 0.0 reduce-scatter.2.cloned.1.call-update
  109.3 2.8 collective-permute-start
  112.1 0.3 collective-permute-start.1
  112.4 2.7 collective-permute-start.2
  115.8 11.5 %collective-permute-done = bf16[320,1024]{1,0:T(8,128)(2,1)} collective-permute-done((bf16[320,1024]{1,0:T(8,128)(2,1)}, bf16[320,1024]{1,0:T(8,128)(2,1)}, u32[]{:S(2)}, u32[]{:S(2)}) %collective-permute-start) | collective-permute-done | bytes 655392 | tf_op jit(solution)/shard_map/ppermute | solution.py:15
  127.3 14.1 %collective-permute-done.1 = bf16[320,1024]{1,0:T(8,128)(2,1)} collective-permute-done((bf16[320,1024]{1,0:T(8,128)(2,1)}, bf16[320,1024]{1,0:T(8,128)(2,1)}, u32[]{:S(2)}, u32[]{:S(2)}) %collective-permute-start.1) | collective-permute-done | bytes 655392 | tf_op jit(solution)/shard_map/ppermute | solution.py:15
  141.4 0.0 collective-permute-done.2
  141.4 201.6 %reduce-scatter.2.cloned.1.call-done = f32[320,1024]{1,0:T(8,128)} async-done(((f32[5120,1024]{1,0:T(8,128)}), f32[320,1024]{1,0:T(8,128)}) %reduce-scatter.2.cloned.1.call-update) | async-done | bytes 1310736 | tf_op jit(solution)/shard_map/reduce_scatter | solution.py:31
  342.9 0.0 copy-done
  342.9 0.0 copy-done.1
  342.9 0.0 copy-done.2
  342.9 3.8 %fusion.17 = (f32[1,320,1024]{2,1,0:T(8,128)}, f32[320,1024]{1,0:T(8,128)}) fusion(f32[1,320,1024]{2,1,0:T(8,128)S(1)} %copy-done.1, bf16[320,1024]{1,0:T(8,128)(2,1)} %collective-permute-done, bf16[320,1024]{1,0:T(8,128)(2,1)} %collective-permute-done.1, bf16[320,1024]{1,0:T(8,128)(2,1)} %collective-permute-done.2, pred[]{:T(512)S(6)} %eq.13, pred[]{:T(512)S(6)} %eq.12, ...), kind=kLoop, calls=%fused_computation.19 | loop fusion | flops 4915200 | bytes 9175043 | tf_op jit(solution)/shard_map/broadcast_in_dim | solution.py:50
  (1 shorter events, 0.0 us)
Async XLA Ops:
  7.2 68.2 %all-gather.3.cloned.1.call-start = ((), (), s32[]{:S(2)}) async-start(), calls=%async_computation.2 | async-start | bytes 11141120 | tf_op jit(solution)/shard_map/all_gather | solution.py:26
  7.9 67.5 %copy-start.4 = (f32[5120]{0:T(1024)S(1)}, f32[5120]{0:T(1024)}, u32[]{:S(2)}) copy-start(f32[5120]{0:T(1024)} %param.11) | copy-start | bytes 61444
  7.9 335.0 %reduce-scatter.2.cloned.1.call-start = ((), (), s32[]{:S(2)}) async-start(), calls=%async_computation.1 | async-start | bytes 22282240 | tf_op jit(solution)/shard_map/reduce_scatter | solution.py:31
  14.0 76.9 %copy-start.3 = (bf16[1,1024,1024]{2,1,0:T(8,128)(2,1)S(1)}, bf16[1,1024,1024]{2,1,0:T(8,128)(2,1)}, u32[]{:S(2)}) copy-start(bf16[1,1024,1024]{2,1,0:T(8,128)(2,1)} %param.10) | copy-start | bytes 6291460
  109.2 233.7 %copy-start = (bf16[1,320,1024]{2,1,0:T(8,128)(2,1)S(1)}, bf16[1,320,1024]{2,1,0:T(8,128)(2,1)}, u32[]{:S(2)}) copy-start(bf16[1,320,1024]{2,1,0:T(8,128)(2,1)} %param.12) | copy-start | bytes 1966084
  109.3 233.7 %copy-start.1 = (f32[1,320,1024]{2,1,0:T(8,128)S(1)}, f32[1,320,1024]{2,1,0:T(8,128)}, u32[]{:S(2)}) copy-start(f32[1,320,1024]{2,1,0:T(8,128)} %param.14) | copy-start | bytes 3932164
  109.3 233.7 %copy-start.2 = (f32[1,320,1024]{2,1,0:T(8,128)S(1)}, f32[1,320,1024]{2,1,0:T(8,128)}, u32[]{:S(2)}) copy-start(f32[1,320,1024]{2,1,0:T(8,128)} %param.15) | copy-start | bytes 3932164
  109.3 18.0 %collective-permute-start = (bf16[320,1024]{1,0:T(8,128)(2,1)}, bf16[320,1024]{1,0:T(8,128)(2,1)}, u32[]{:S(2)}, u32[]{:S(2)}) collective-permute-start(bf16[320,1024]{1,0:T(8,128)(2,1)} %bitcast.33), channel_id=1, source_target_pairs={{0,64},{16,80},{32,96},{48,112},{64,0},{80,16},{96,32},{112,48},{1... | collective-permute-start | bytes 1966088 | tf_op jit(solution)/shard_map/ppermute | solution.py:15
  112.1 29.3 %collective-permute-start.1 = (bf16[320,1024]{1,0:T(8,128)(2,1)}, bf16[320,1024]{1,0:T(8,128)(2,1)}, u32[]{:S(2)}, u32[]{:S(2)}) collective-permute-start(bf16[320,1024]{1,0:T(8,128)(2,1)} %bitcast.34), channel_id=1, source_target_pairs={{0,32},{16,48},{32,0},{48,16},{64,96},{80,112},{96,64},{112,80},{1... | collective-permute-start | bytes 1966088 | tf_op jit(solution)/shard_map/ppermute | solution.py:15
  112.4 29.0 %collective-permute-start.2 = (bf16[320,1024]{1,0:T(8,128)(2,1)}, bf16[320,1024]{1,0:T(8,128)(2,1)}, u32[]{:S(2)}, u32[]{:S(2)}) collective-permute-start(bf16[320,1024]{1,0:T(8,128)(2,1)} %bitcast.35), channel_id=1, source_target_pairs={{0,16},{16,0},{32,48},{48,32},{64,80},{80,64},{96,112},{112,96},{1... | collective-permute-start | bytes 1966088 | tf_op jit(solution)/shard_map/ppermute | solution.py:15
Sparse Core Ops, SparseCore 0:
  9.7 65.6 all-gather.2
  109.4 233.4 reduce-scatter.1
where the time goes:
time: 355 us; the launch traced here: 354 us
  waiting for transfers between devices  289 us (81%)
  matrix products  33.8 us (10%)
  between operations  14.7 us (4%)
  other arithmetic  9.92 us (3%)
  starting transfers between devices  5.9 us (2%)
    reduce_scatter x1, waiting for transfers between devices, shards(): lax.psum_scatter(lax.dot_general(columns, error, (((0,), (0,)), ((), ()))...  202 us
    all_gather x1, waiting for transfers between devices, shards(): lax.all_gather(weights[0], 'fsdp', axis=0, tiled=True)  61.3 us
    ppermute x3, waiting for transfers between devices, swapped(): return lax.ppermute(value, axis, pairs)  25.6 us
    dot_general x1, matrix products, shards(): lax.dot_general(columns, error, (((0,), (0,)), ((), ())), preferred_eleme...  18.3 us
    dot_general x1, matrix products, shards(): jnp.dot(columns, lax.all_gather(weights[0], 'fsdp', axis=0, tiled=True),...  15.5 us
  transfers between devices with their start and end apart: 5, of which 4 were waited for; matrix products, arithmetic and copies ran while one was open for 2% of the time, Pallas kernels for 0%

commit v1 on v0

v1 whole, which is shorter than its diff:
```python
import functools

import jax
import jax.numpy as jnp
from jax import lax
from jax.experimental import pallas as pl
from jax.experimental.pallas import tpu as pltpu
from jax.sharding import PartitionSpec as P

EPS = 1e-06
INNER_RATE = 0.05
OUTER_RATE = 1.0
SLOW_BETA = 0.6

MESH = pl.DeviceIdType.MESH
BF16 = jnp.bfloat16
F32 = jnp.float32

ROWS = 320
BLOCK = 2 * ROWS
CHUNK = 256
CHUNKS = 2
TILE = 128
STEP = 512
N_AG = 15
N_RS = 26


def kernel(
    mask,
    p_rows,
    tokens,
    target,
    gain,
    weights,
    previous,
    anchor,
    momentum,
    new_momentum,
    new_anchor,
    normed,
    full,
    grad,
    grad_half,
    tgt,
    err,
    from_mate,
    far,
    near,
    mate_p,
    total,
    swapped,
    own_w,
    partner,
    anchor_v,
    momentum_v,
    gain_v,
    ag_send,
    ag_recv,
    rs_send,
    rs_recv,
    n_send,
    n_recv,
    m_send,
    m_recv,
    local,
):
    rep = lax.axis_index("rep")
    at = lax.axis_index("fsdp")
    core = lax.rem(at, 2)
    other = 1 - core
    x = lax.rem(at // 2, 2)
    z = at // 4
    z_up, z_down, z_far = lax.rem(z + 1, 4), lax.rem(z + 3, 4), lax.rem(z + 2, 4)
    up = (rep, z_up * 4 + x * 2 + core)
    down = (rep, z_down * 4 + x * 2 + core)
    mate = (rep, z * 4 + (1 - x) * 2 + core)
    sibling = (rep, z * 4 + x * 2 + other)
    friend = (rep + mask - 2 * mask * lax.rem(rep // mask, 2), at)

    tokens_here, width = tokens.shape
    scale = width ** (-0.5)
    half = p_rows // 2
    q_rows = BLOCK - p_rows
    PA, PB = (0, half), (BLOCK - half, half)
    QA, QB, Q = (half, q_rows // 2), (ROWS, q_rows // 2), (half, q_rows)
    H0, H1, ALL = (0, ROWS), (ROWS, ROWS), (0, BLOCK)

    def remote(src, dst, send, recv, device):
        return pltpu.make_async_remote_copy(
            src_ref=src,
            dst_ref=dst,
            send_sem=send,
            recv_sem=recv,
            device_id=device,
            device_id_type=MESH,
        )

    sent = []

    def load(src, dst, i):
        copy = pltpu.make_async_copy(src, dst, local.at[i])
        copy.start()
        return copy

    def cols(c, j):
        return pl.ds(pl.multiple_of(c * CHUNKS * CHUNK + j * CHUNK, CHUNK), CHUNK)

    def half_cols(c):
        return pl.ds(pl.multiple_of(c * CHUNKS * CHUNK, CHUNK), CHUNKS * CHUNK)

    own_start = (z * 2 + x) * BLOCK

    def own_rows(c):
        return pl.ds(pl.multiple_of(own_start + c * ROWS, 64), ROWS)

    w_loads = [
        load(weights.at[:, cols(core, j)], full.at[j, own_rows(core)], j)
        for j in range(CHUNKS)
    ]
    tiles = tokens_here // TILE

    def tile_of(c, i):
        return pl.ds(pl.multiple_of(c * tokens_here + i * TILE, TILE), TILE)

    gain_load = load(gain, gain_v, 2)
    token_base = 8

    @pl.loop(0, tiles)
    def _(i):
        rows = pl.ds(pl.multiple_of(i * TILE, TILE), TILE)
        pltpu.make_async_copy(
            tokens.at[rows], normed.at[tile_of(core, i)], local.at[token_base + i]
        ).start()

    tgt_load = load(target.at[:, half_cols(core)], tgt.at[core], 3)
    own_w_load = load(weights, own_w, 4)
    anchor_load = load(anchor, anchor_v, 5)
    momentum_load = load(momentum, momentum_v, 6)

    barrier = pltpu.get_barrier_semaphore()
    for device in (up, down, mate, sibling, friend):
        pl.semaphore_signal(barrier, inc=1, device_id=device, device_id_type=MESH)
    pl.semaphore_wait(barrier, 5)

    def w_swap(j):
        return remote(
            weights.at[:, cols(other, j)],
            full.at[j, own_rows(core)],
            m_send.at[j],
            m_recv.at[j],
            sibling,
        )

    for j in range(CHUNKS):
        w_swap(j).start()
    tgt_swap = remote(
        target.at[:, half_cols(other)], tgt.at[core], m_send.at[2], m_recv.at[2], sibling
    )
    friend_swap = remote(previous, partner, m_send.at[3], m_recv.at[3], friend)

    def piece(j, zz, xx, part):
        start = pl.multiple_of((zz * 2 + xx) * BLOCK + part[0], 16)
        return full.at[j, pl.ds(start, part[1])]

    def ag_copy(j, i, zz, xx, part, device):
        where = piece(j, zz, xx, part)
        return remote(where, where, ag_send.at[j, i], ag_recv.at[j, i], device)

    def ag_start(j, i, zz, xx, part, device):
        ag_copy(j, i, zz, xx, part, device).start()
        sent.append(lambda: ag_copy(j, i, zz, xx, part, device))

    def ag_wait(j, i, zz, xx, part):
        ag_copy(j, i, zz, xx, part, mate).wait_recv()

    xm = 1 - x

    def gather_own(j):
        w_loads[j].wait()
        pltpu.make_async_copy(
            full.at[j, own_rows(other)], full.at[j, own_rows(other)], m_recv.at[j]
        ).wait()
        ag_start(j, 0, z, x, ALL, mate)
        ag_start(j, 1, z, x, ALL, up)
        ag_start(j, 2, z, x, ALL, down)

    def gather_1(j):
        ag_wait(j, 0, z, xm, ALL)
        ag_start(j, 3, z, xm, PA, up)
        ag_start(j, 6, z, xm, PB, down)
        ag_start(j, 4, z, xm, PB, up)
        ag_start(j, 5, z, xm, PA, down)
        ag_wait(j, 1, z_down, x, ALL)
        ag_start(j, 7, z_down, x, H0, up)
        ag_start(j, 8, z_down, x, Q, mate)
        ag_wait(j, 2, z_up, x, ALL)
        ag_start(j, 9, z_up, x, H1, down)
        ag_start(j, 10, z_up, x, Q, mate)

    def gather_2(j):
        ag_wait(j, 3, z_down, xm, PA)
        ag_start(j, 11, z_down, xm, PA, up)
        ag_wait(j, 6, z_up, xm, PB)
        ag_start(j, 12, z_up, xm, PB, down)

    def gather_3(j):
        ag_wait(j, 7, z_far, x, H0)
        ag_start(j, 13, z_far, x, QA, mate)
        ag_wait(j, 9, z_far, x, H1)
        ag_start(j, 14, z_far, x, QB, mate)

    def gather_4(j):
        ag_wait(j, 4, z_down, xm, PB)
        ag_wait(j, 5, z_up, xm, PA)
        ag_wait(j, 8, z_down, xm, Q)
        ag_wait(j, 10, z_up, xm, Q)
        ag_wait(j, 11, z_far, xm, PA)
        ag_wait(j, 12, z_far, xm, PB)
        ag_wait(j, 13, z_far, xm, QA)
        ag_wait(j, 14, z_far, xm, QB)

    def tile_copy(c, i):
        where = normed.at[tile_of(c, i)]
        return remote(where, where, n_send.at[i], n_recv.at[i], sibling)

    def norm_tile(i):
        where = tile_of(core, i)
        pltpu.make_async_copy(
            normed.at[where], normed.at[where], local.at[token_base + i]
        ).wait()
        for part in range(2):
            rows = pl.ds(
                pl.multiple_of(core * tokens_here + i * TILE + part * (TILE // 2), 64),
                TILE // 2,
            )
            value = normed[rows, :].astype(F32)
            rms = lax.rsqrt(jnp.mean(value * value, axis=-1, keepdims=True) + EPS)
            normed[rows, :] = (value * rms * gain_v[...]).astype(BF16)
        tile_copy(core, i).start()

    steps = tokens_here // STEP

    def values_step(j, s):
        side = jnp.where(s < steps, core, other)
        inner = lax.rem(s, steps) * STEP
        rows = pl.ds(pl.multiple_of(side * tokens_here + inner, STEP), STEP)
        values = jnp.dot(normed[rows, :], full[j], preferred_element_type=F32) * scale
        goal = tgt[
            side, pl.ds(pl.multiple_of(inner, STEP), STEP), j * CHUNK : (j + 1) * CHUNK
        ].astype(F32)
        err[rows, :] = (values - goal).astype(BF16)

    def grad_step(j, s):
        i = s // 2
        dz = jnp.where(i == 0, 2, jnp.where(i == 1, 1, jnp.where(i == 2, 3, 0)))
        block = lax.rem(z + dz, 4) * 2 + jnp.where(lax.rem(s, 2) == 0, 1 - x, x)
        where = pl.ds(pl.multiple_of(block * BLOCK, 128), BLOCK)
        part = lax.dot_general(
            normed[:, where], err[...], (((0,), (0,)), ((), ())), preferred_element_type=F32
        )
        grad[j, s] = part
        grad_half[j, s] = part.astype(BF16)

    def rs_copy(j, i, src, dst, device):
        return remote(src, dst, rs_send.at[j, i], rs_recv.at[j, i], device)

    def rs_start(j, i, src, dst, device):
        rs_copy(j, i, src, dst, device).start()
        is_total, count = src.dtype == F32, src.shape[0]

        def again():
            where = (total if is_total else grad_half.at[j]).at[0, pl.ds(0, count)]
            return rs_copy(j, i, where, where, mate)

        sent.append(again)

    def rs_wait(j, i, dst):
        rs_copy(j, i, dst, dst, mate).wait_recv()

    def out_of(j, s, part):
        return grad_half.at[j, s, pl.ds(*part)]

    far_p = ((0, half), (half, half))
    far_q = (2 * half, q_rows // 2)
    mate_pa, mate_pb = (BLOCK, half), (BLOCK + half, half)

    def near_at(j, d, part):
        return near.at[j, d, pl.ds(*part)]

    def far_at(j, d, part):
        return far.at[j, d, pl.ds(*part)]

    def scatter_q(j, i):
        rs_start(j, i, out_of(j, 2 * i, Q), from_mate.at[j, i], mate)

    def scatter_far(j):
        for c in range(2):
            rs_start(j, 4 + c, out_of(j, c, PA), far_at(j, 0, far_p[c]), up)
            rs_start(j, 6 + c, out_of(j, c, PB), far_at(j, 1, far_p[c]), down)

    def scatter_up(j):
        rs_start(j, 8, out_of(j, 2, PB), near_at(j, 0, mate_pb), up)
        rs_start(j, 9, out_of(j, 3, PB), near_at(j, 0, PB), up)

    def scatter_down(j):
        rs_start(j, 10, out_of(j, 4, PA), near_at(j, 1, mate_pa), down)
        rs_start(j, 11, out_of(j, 5, PA), near_at(j, 1, PA), down)

    def add_and_send(j, s, part, terms, i, dst, device):
        where = pl.ds(*part)
        value = grad[j, s, where, :]
        for term in terms:
            value = value + term[...].astype(F32)
        grad_half[j, s, where, :] = value.astype(BF16)
        rs_start(j, i, out_of(j, s, part), dst, device)

    def relay_p(j):
        for c in range(2):
            rs_wait(j, 4 + c, far_at(j, 0, far_p[c]))
            dst = near_at(j, 0, PA if c else mate_pa)
            add_and_send(j, 2 + c, PA, [far_at(j, 0, far_p[c])], 12 + c, dst, up)
            rs_wait(j, 6 + c, far_at(j, 1, far_p[c]))
            dst = near_at(j, 1, PB if c else mate_pb)
            add_and_send(j, 4 + c, PB, [far_at(j, 1, far_p[c])], 14 + c, dst, down)

    def mate_q(j, i, lower):
        start, count = (0, q_rows // 2) if lower else (q_rows // 2, q_rows // 2)
        return from_mate.at[j, i, pl.ds(start, count)]

    def far_q_send(j):
        rs_wait(j, 0, from_mate.at[j, 0])
        add_and_send(j, 1, QA, [mate_q(j, 0, True)], 16, far_at(j, 0, far_q), up)
        add_and_send(j, 1, QB, [mate_q(j, 0, False)], 17, far_at(j, 1, far_q), down)

    def near_q_up(j):
        rs_wait(j, 1, from_mate.at[j, 1])
        add_and_send(j, 3, QB, [mate_q(j, 1, False)], 18, near_at(j, 0, QB), up)

    def near_q_down(j):
        rs_wait(j, 2, from_mate.at[j, 2])
        add_and_send(j, 5, QA, [mate_q(j, 2, True)], 19, near_at(j, 1, QA), down)

    def relay_q(j):
        rs_wait(j, 16, far_at(j, 0, far_q))
        terms = [mate_q(j, 1, True), far_at(j, 0, far_q)]
        add_and_send(j, 3, QA, terms, 20, near_at(j, 0, QA), up)
        rs_wait(j, 17, far_at(j, 1, far_q))
        terms = [mate_q(j, 2, False), far_at(j, 1, far_q)]
        add_and_send(j, 5, QB, terms, 21, near_at(j, 1, QB), down)

    def mate_send(j):
        rs_wait(j, 12, near_at(j, 0, mate_pa))
        rs_wait(j, 10, near_at(j, 1, mate_pa))
        terms = [near_at(j, 0, mate_pa), near_at(j, 1, mate_pa)]
        add_and_send(j, 6, PA, terms, 22, mate_p.at[j, 0], mate)
        rs_wait(j, 8, near_at(j, 0, mate_pb))
        rs_wait(j, 14, near_at(j, 1, mate_pb))
        terms = [near_at(j, 0, mate_pb), near_at(j, 1, mate_pb)]
        add_and_send(j, 6, PB, terms, 23, mate_p.at[j, 1], mate)

    def finish(j):
        def put(part, terms):
            where = pl.ds(*part)
            value = grad[j, 7, where, :]
            for term in terms:
                value = value + term[...].astype(F32)
            total[j, where, :] = value

        rs_wait(j, 3, from_mate.at[j, 3])
        rs_wait(j, 13, near_at(j, 0, PA))
        rs_wait(j, 11, near_at(j, 1, PA))
        rs_wait(j, 22, mate_p.at[j, 0])
        put(PA, [near_at(j, 0, PA), near_at(j, 1, PA), mate_p.at[j, 0]])
        rs_wait(j, 9, near_at(j, 0, PB))
        rs_wait(j, 15, near_at(j, 1, PB))
        rs_wait(j, 23, mate_p.at[j, 1])
        put(PB, [near_at(j, 0, PB), near_at(j, 1, PB), mate_p.at[j, 1]])
        rs_wait(j, 20, near_at(j, 0, QA))
        rs_wait(j, 19, near_at(j, 1, QA))
        put(QA, [near_at(j, 0, QA), near_at(j, 1, QA), mate_q(j, 3, True)])
        rs_wait(j, 18, near_at(j, 0, QB))
        rs_wait(j, 21, near_at(j, 1, QB))
        put(QB, [near_at(j, 0, QB), near_at(j, 1, QB), mate_q(j, 3, False)])
        theirs = pl.ds(pl.multiple_of(other * ROWS, 64), ROWS)
        rs_start(j, 24, total.at[j, theirs], swapped.at[j], sibling)

    def update(columns, gradient):
        fast = own_w[:, columns].astype(F32) - INNER_RATE * (gradient * scale)
        mixed = 0.5 * fast + 0.5 * partner[:, columns].astype(F32)
        base = anchor_v[:, columns]
        moment = SLOW_BETA * momentum_v[:, columns] + (base - mixed) / INNER_RATE
        new_momentum[:, columns] = moment
        new_anchor[:, columns] = base - OUTER_RATE * INNER_RATE * moment

    def update_own(j):
        mine = pl.ds(pl.multiple_of(core * ROWS, 64), ROWS)
        update(cols(core, j), total[j, mine, :])

    def update_other(j):
        rs_wait(j, 24, swapped.at[j])
        update(cols(other, j), swapped[j])

    gather_own(0)
    gain_load.wait()

    @pl.loop(0, tiles)
    def _(i):
        norm_tile(i)

    tgt_swap.start()
    gather_1(0)
    gather_2(0)
    gather_own(1)
    friend_swap.start()
    gather_3(0)
    gather_4(0)
    tgt_load.wait()

    @pl.loop(0, steps)
    def _(s):
        values_step(0, s)

    gather_1(1)
    pltpu.make_async_copy(tgt.at[other], tgt.at[other], m_recv.at[2]).wait()

    @pl.loop(0, tiles)
    def _(i):
        tile_copy(other, i).wait_recv()

    @pl.loop(steps, 2 * steps)
    def _(s):
        values_step(0, s)

    gather_2(1)

    @pl.loop(0, 8)
    def _(s):
        grad_step(0, s)

        @pl.when(s == 3)
        def _():
            gather_3(1)

    def scatter_begin(j):
        scatter_far(j)
        scatter_q(j, 0)
        scatter_q(j, 1)
        scatter_up(j)
        scatter_q(j, 2)
        scatter_down(j)
        scatter_q(j, 3)

    scatter_begin(0)
    gather_4(1)

    @pl.loop(0, 2 * steps)
    def _(s):
        values_step(1, s)

    relay_p(0)
    far_q_send(0)

    @pl.loop(0, 8)
    def _(s):
        grad_step(1, s)

        @pl.when(s == 3)
        def _():
            near_q_up(0)
            near_q_down(0)

    scatter_begin(1)
    relay_q(0)
    mate_send(0)
    friend_swap.wait_recv()
    own_w_load.wait()
    anchor_load.wait()
    momentum_load.wait()
    relay_p(1)
    far_q_send(1)
    finish(0)
    near_q_up(1)
    near_q_down(1)
    update_own(0)
    mate_send(1)
    relay_q(1)
    update_other(0)
    finish(1)
    update_own(1)
    update_other(1)

    for j in range(CHUNKS):
        w_swap(j).wait_send()
    tgt_swap.wait_send()
    friend_swap.wait_send()

    @pl.loop(0, tiles)
    def _(i):
        tile_copy(core, i).wait_send()

    for copy in sent:
        copy().wait_send()


def run(mask, p_rows, collective_id, tokens, target, gain, weights, previous, anchor, momentum):
    rows, width = tokens.shape
    kv = target.shape[1]
    half, q_rows = p_rows // 2, BLOCK - p_rows
    anywhere = pl.BlockSpec(memory_space=pl.ANY)
    here = pl.BlockSpec(memory_space=pltpu.VMEM)
    vmem, dma = pltpu.VMEM, pltpu.SemaphoreType.DMA
    side = CHUNKS * CHUNK
    return pl.pallas_call(
        functools.partial(kernel, mask, p_rows),
        out_shape=(
            jax.ShapeDtypeStruct((ROWS, kv), F32),
            jax.ShapeDtypeStruct((ROWS, kv), F32),
        ),
        in_specs=[anywhere] * 7,
        out_specs=(here, here),
        scratch_shapes=[
            vmem((2 * rows, width), BF16),
            vmem((CHUNKS, width, CHUNK), BF16),
            vmem((CHUNKS, 8, BLOCK, CHUNK), F32),
            vmem((CHUNKS, 8, BLOCK, CHUNK), BF16),
            vmem((2, rows, side), BF16),
            vmem((2 * rows, CHUNK), BF16),
            vmem((CHUNKS, 4, q_rows, CHUNK), BF16),
            vmem((CHUNKS, 2, p_rows + q_rows // 2, CHUNK), BF16),
            vmem((CHUNKS, 2, BLOCK + p_rows, CHUNK), BF16),
            vmem((CHUNKS, 2, half, CHUNK), BF16),
            vmem((CHUNKS, BLOCK, CHUNK), F32),
            vmem((CHUNKS, ROWS, CHUNK), F32),
            vmem((ROWS, kv), BF16),
            vmem((ROWS, kv), BF16),
            vmem((ROWS, kv), F32),
            vmem((ROWS, kv), F32),
            vmem((1, width), F32),
            dma((CHUNKS, N_AG)),
            dma((CHUNKS, N_AG)),
            dma((CHUNKS, N_RS)),
            dma((CHUNKS, N_RS)),
            dma((rows // TILE,)),
            dma((rows // TILE,)),
            dma((4,)),
            dma((4,)),
            dma((8 + rows // TILE,)),
        ],
        compiler_params=pltpu.CompilerParams(
            collective_id=collective_id,
            has_side_effects=True,
            vmem_limit_bytes=63 << 20,
        ),
    )(tokens, target, gain, weights, previous, anchor, momentum)


def shards(step_bit, tokens, target, norm_gain, weights, previous, anchor, momentum):
    bit_count = lax.axis_size("rep").bit_length() - 1
    chosen_bit = jnp.remainder(step_bit, jnp.int32(bit_count))
    branches = [
        functools.partial(run, 2**bit, 416 if bit == 0 else 352, bit)
        for bit in range(bit_count)
    ]
    moment_new, anchor_new = lax.switch(
        chosen_bit,
        branches,
        tokens[0],
        target[0],
        norm_gain[None],
        weights[0],
        previous[0],
        anchor[0],
        momentum[0],
    )
    return (moment_new[None], anchor_new[None])


def solution(mesh):
    placed = (
        P(),
        P("rep", "fsdp", None),
        P("rep", "fsdp", None),
        P(),
        P("rep", "fsdp", None),
        P("rep", "fsdp", None),
        P("rep", "fsdp", None),
        P("rep", "fsdp", None),
    )
    return jax.shard_map(
        shards,
        mesh=mesh,
        in_specs=placed,
        out_specs=(P("rep", "fsdp", None), P("rep", "fsdp", None)),
        check_vma=False,
    )
```

time: 355 us -> 101 us (0.28)
  waiting for transfers between devices: 289 us -> 0 us
  Pallas kernels: 0 us -> 94.1 us
  matrix products: 33.8 us -> 0 us
  between operations: 14.7 us -> 1.31 us
  other arithmetic: 9.92 us -> 0 us
  starting transfers between devices: 5.9 us -> 0 us
  local copies, waits for them, and re-layouts: 0.02 us -> 3.69 us
    reduce_scatter x1 -> x0, waiting for transfers between devices: 202 us -> none  [shards(): lax.psum_scatter(lax.dot_general(columns, error, (((0,), (0,)), ((), ()))...]
    pallas_call x0 -> x1, Pallas kernels: none -> 94.1 us  [run(): pl.pallas_call(functools.partial(kernel, mask, p_rows), out_shape=(jax.Sh...]
    all_gather x1 -> x0, waiting for transfers between devices: 61.3 us -> none  [shards(): lax.all_gather(weights[0], 'fsdp', axis=0, tiled=True)]
    dot_general x2 -> x0, matrix products: 33.8 us -> none  [the longest x1 18.3 us: shards(): lax.dot_general(columns, error, (((0,), (0,)), ((), ())), preferred_eleme...]
    ppermute x3 -> x0, waiting for transfers between devices: 25.6 us -> none  [swapped(): return lax.ppermute(value, axis, pairs)]
    reduce_sum x1 -> x0, other arithmetic: 6.08 us -> none  [shards(): jnp.mean(token_rows * token_rows, axis=-1, keepdims=True) + EPS]
    ppermute x3 -> x0, starting transfers between devices: 5.82 us -> none  [swapped(): return lax.ppermute(value, axis, pairs)]
    broadcast_in_dim x1 -> x0, other arithmetic: 3.84 us -> none  [shards(): return (moment_new[None], anchor_new[None])]
  transfers between devices with their start and end apart: 5 -> 0, of which waited for: 4 -> 0; matrix products, arithmetic and copies ran while one was open for 2% -> 0% of each run, Pallas kernels for 0% -> 0%
where the time goes in v1:
time: 101 us; the launch traced here: 99.8 us
  Pallas kernels  94.1 us (93%)
  local copies, waits for them, and re-layouts  3.69 us (4%)
  between operations  1.31 us (1%)
    pallas_call x1, Pallas kernels, run(): pl.pallas_call(functools.partial(kernel, mask, p_rows), out_shape=(jax.Sh...  94.1 us
    unnamed x4, local copies, waits for them, and re-layouts  3.69 us

profile of v1, /device:TPU:1, one launch (start us, length us, event | category | flops | bytes accessed | tf_op | source)
XLA Modules:
  0.0 99.8 jit_solution(9444878537321449057)
XLA Ops:
  1.3 94.8 %conditional.1 = ((f32[320,1024]{1,0:T(8,128)}, f32[320,1024]{1,0:T(8,128)})) conditional(s32[]{:T(128)} %clamp.3, (bf16[1024,5120]{1,0:T(8,128)(2,1)}, bf16[1024,1024]{1,0:T(8,128)(2,1)}, f32[1,5120]{1,0:T(1,128)}, bf16[320,1024]{1,0:T(8,128)(2,1)}, bf16[320,1024]{1,0:T(8,128)(2,1)}, /*index=5*/f32[320,1024]{1,0:T(8,128)}, ...), branch_computations={%region_0.1_spmd, %region_1.2_spmd, %region_2.3_spmd} | conditional | bytes 8 | solution.py:565
  1.7 94.1 %branch_2_fun.1 = (f32[320,1024]{1,0:T(8,128)}, f32[320,1024]{1,0:T(8,128)}) custom-call(bf16[1024,5120]{1,0:T(8,128)(2,1)} %get-tuple-element.68.tokens, bf16[1024,1024]{1,0:T(8,128)(2,1)} %get-tuple-element.69.target, f32[1,5120]{1,0:T(1,128)} %get-tuple-element.70.gain, bf16[320,1024]{1,0:T(8,128)(2,1)} %get-tuple-element.71.weights, ...), custom_call_target="tpu_custom_call" | custom-call | tf_op jit(solution)/shard_map/cond/branch_2_fun/pallas_call | solution.py:514
  96.1 0.0 copy-start
  96.1 2.6 %copy.19 = f32[1,320,1024]{2,1,0:T(8,128)} copy(f32[1,320,1024]{2,1,0:T(8,128)} %bitcast.27) | data formatting | bytes 2621440
  98.7 0.0 copy-done
  98.7 1.1 %copy.20 = f32[1,320,1024]{2,1,0:T(8,128)} copy(f32[1,320,1024]{2,1,0:T(8,128)S(1)} %bitcast.28) | data formatting | bytes 2621440
Async XLA Ops:
  96.1 2.6 %copy-start = (f32[320,1024]{1,0:T(8,128)S(1)}, f32[320,1024]{1,0:T(8,128)}, u32[]{:S(2)}) copy-start(f32[320,1024]{1,0:T(8,128)} %get-tuple-element.80) | copy-start | bytes 3932164

commit v2 on v1

--- a/solution.py
+++ b/solution.py
@@ -20,9 +20,10 @@
 BLOCK = 2 * ROWS
 CHUNK = 256
 CHUNKS = 2
+FRIEND_PARTS = 4
 TILE = 128
 STEP = 512
-N_AG = 15
+N_AG = 18
 N_RS = 26
 
 
@@ -72,9 +73,9 @@
     x = lax.rem(at // 2, 2)
     z = at // 4
     z_up, z_down, z_far = lax.rem(z + 1, 4), lax.rem(z + 3, 4), lax.rem(z + 2, 4)
-    up = (rep, z_up * 4 + x * 2 + core)
-    down = (rep, z_down * 4 + x * 2 + core)
-    mate = (rep, z * 4 + (1 - x) * 2 + core)
+    up, up_other = [(rep, z_up * 4 + x * 2 + c) for c in (core, other)]
+    down, down_other = [(rep, z_down * 4 + x * 2 + c) for c in (core, other)]
+    mate, mate_other = [(rep, z * 4 + (1 - x) * 2 + c) for c in (core, other)]
     sibling = (rep, z * 4 + x * 2 + other)
     friend = (rep + mask - 2 * mask * lax.rem(rep // mask, 2), at)
 
@@ -109,10 +110,10 @@
     def half_cols(c):
         return pl.ds(pl.multiple_of(c * CHUNKS * CHUNK, CHUNK), CHUNKS * CHUNK)
 
-    own_start = (z * 2 + x) * BLOCK
+    own_base = (z * 2 + x) * BLOCK
 
     def own_rows(c):
-        return pl.ds(pl.multiple_of(own_start + c * ROWS, 64), ROWS)
+        return pl.ds(pl.multiple_of(own_base + c * ROWS, 64), ROWS)
 
     w_loads = [
         load(weights.at[:, cols(core, j)], full.at[j, own_rows(core)], j)
@@ -139,9 +140,10 @@
     momentum_load = load(momentum, momentum_v, 6)
 
     barrier = pltpu.get_barrier_semaphore()
-    for device in (up, down, mate, sibling, friend):
+    everyone = (up, up_other, down, down_other, mate, mate_other, sibling, friend)
+    for device in everyone:
         pl.semaphore_signal(barrier, inc=1, device_id=device, device_id_type=MESH)
-    pl.semaphore_wait(barrier, 5)
+    pl.semaphore_wait(barrier, len(everyone))
 
     def w_swap(j):
         return remote(
@@ -151,13 +153,16 @@
             m_recv.at[j],
             sibling,
         )
-
-    for j in range(CHUNKS):
-        w_swap(j).start()
     tgt_swap = remote(
         target.at[:, half_cols(other)], tgt.at[core], m_send.at[2], m_recv.at[2], sibling
     )
-    friend_swap = remote(previous, partner, m_send.at[3], m_recv.at[3], friend)
+    friend_rows = ROWS // FRIEND_PARTS
+
+    def friend_swap(i):
+        where = pl.ds(i * friend_rows, friend_rows)
+        return remote(
+            previous.at[where], partner.at[where], m_send.at[3 + i], m_recv.at[3 + i], friend
+        )
 
     def piece(j, zz, xx, part):
         start = pl.multiple_of((zz * 2 + xx) * BLOCK + part[0], 16)
@@ -176,49 +181,71 @@
 
     xm = 1 - x
 
-    def gather_own(j):
+    def own_copy(j, i, c, device):
+        return remote(
+            weights.at[:, cols(c, j)],
+            full.at[j, own_rows(core)],
+            ag_send.at[j, i + jnp.where(c == core, 0, 1)],
+            ag_recv.at[j, i + core],
+            device,
+        )
+
+    def own_start(j, i, same, cross):
+        for c, device in ((core, same), (other, cross)):
+            own_copy(j, i, c, device).start()
+            sent.append(lambda c=c, device=device: own_copy(j, i, c, device))
+
+    def own_wait(j, i, zz, xx, h):
+        where = piece(j, zz, xx, (H0, H1)[h])
+        remote(where, where, ag_send.at[j, i], ag_recv.at[j, i + h], mate).wait_recv()
+
+    def gather_own_z(j):
+        own_start(j, 2, up, up_other)
+        own_start(j, 4, down, down_other)
+
+    def gather_own_x(j):
+        own_start(j, 0, mate, mate_other)
+        w_swap(j).start()
+
+    def gather_1(j):
+        own_wait(j, 0, z, xm, 0)
+        ag_start(j, 6, z, xm, PA, up)
+        ag_start(j, 8, z, xm, PA, down)
+        own_wait(j, 0, z, xm, 1)
+        ag_start(j, 9, z, xm, PB, down)
+        ag_start(j, 7, z, xm, PB, up)
+        own_wait(j, 2, z_down, x, 0)
+        ag_start(j, 10, z_down, x, H0, up)
+        own_wait(j, 4, z_up, x, 1)
+        ag_start(j, 12, z_up, x, H1, down)
+        own_wait(j, 2, z_down, x, 1)
+        ag_start(j, 11, z_down, x, Q, mate)
+        own_wait(j, 4, z_up, x, 0)
+        ag_start(j, 13, z_up, x, Q, mate)
+
+    def gather_2(j):
+        ag_wait(j, 6, z_down, xm, PA)
+        ag_start(j, 14, z_down, xm, PA, up)
+        ag_wait(j, 9, z_up, xm, PB)
+        ag_start(j, 15, z_up, xm, PB, down)
+
+    def gather_3(j):
+        ag_wait(j, 10, z_far, x, H0)
+        ag_start(j, 16, z_far, x, QA, mate)
+        ag_wait(j, 12, z_far, x, H1)
+        ag_start(j, 17, z_far, x, QB, mate)
+
+    def gather_4(j):
         w_loads[j].wait()
-        pltpu.make_async_copy(
-            full.at[j, own_rows(other)], full.at[j, own_rows(other)], m_recv.at[j]
-        ).wait()
-        ag_start(j, 0, z, x, ALL, mate)
-        ag_start(j, 1, z, x, ALL, up)
-        ag_start(j, 2, z, x, ALL, down)
-
-    def gather_1(j):
-        ag_wait(j, 0, z, xm, ALL)
-        ag_start(j, 3, z, xm, PA, up)
-        ag_start(j, 6, z, xm, PB, down)
-        ag_start(j, 4, z, xm, PB, up)
-        ag_start(j, 5, z, xm, PA, down)
-        ag_wait(j, 1, z_down, x, ALL)
-        ag_start(j, 7, z_down, x, H0, up)
-        ag_start(j, 8, z_down, x, Q, mate)
-        ag_wait(j, 2, z_up, x, ALL)
-        ag_start(j, 9, z_up, x, H1, down)
-        ag_start(j, 10, z_up, x, Q, mate)
-
-    def gather_2(j):
-        ag_wait(j, 3, z_down, xm, PA)
-        ag_start(j, 11, z_down, xm, PA, up)
-        ag_wait(j, 6, z_up, xm, PB)
-        ag_start(j, 12, z_up, xm, PB, down)
-
-    def gather_3(j):
-        ag_wait(j, 7, z_far, x, H0)
-        ag_start(j, 13, z_far, x, QA, mate)
-        ag_wait(j, 9, z_far, x, H1)
-        ag_start(j, 14, z_far, x, QB, mate)
-
-    def gather_4(j):
-        ag_wait(j, 4, z_down, xm, PB)
-        ag_wait(j, 5, z_up, xm, PA)
-        ag_wait(j, 8, z_down, xm, Q)
-        ag_wait(j, 10, z_up, xm, Q)
-        ag_wait(j, 11, z_far, xm, PA)
-        ag_wait(j, 12, z_far, xm, PB)
-        ag_wait(j, 13, z_far, xm, QA)
-        ag_wait(j, 14, z_far, xm, QB)
+        w_swap(j).wait_recv()
+        ag_wait(j, 7, z_down, xm, PB)
+        ag_wait(j, 8, z_up, xm, PA)
+        ag_wait(j, 11, z_down, xm, Q)
+        ag_wait(j, 13, z_up, xm, Q)
+        ag_wait(j, 14, z_far, xm, PA)
+        ag_wait(j, 15, z_far, xm, PB)
+        ag_wait(j, 16, z_far, xm, QA)
+        ag_wait(j, 17, z_far, xm, QB)
 
     def tile_copy(c, i):
         where = normed.at[tile_of(c, i)]
@@ -401,19 +428,35 @@
         rs_wait(j, 24, swapped.at[j])
         update(cols(other, j), swapped[j])
 
-    gather_own(0)
+    def when(s, step, *todo):
+        @pl.when(s == step)
+        def _():
+            for do in todo:
+                do()
+
+    def friend_part(i):
+        if mask == 1:
+            friend_swap(i).start()
+
+    gather_own_x(0)
+    gather_own_z(0)
+    if mask != 1:
+        for i in range(FRIEND_PARTS):
+            friend_swap(i).start()
+    friend_part(0)
+    tgt_swap.start()
     gain_load.wait()
 
     @pl.loop(0, tiles)
     def _(i):
         norm_tile(i)
 
-    tgt_swap.start()
     gather_1(0)
     gather_2(0)
-    gather_own(1)
-    friend_swap.start()
+    gather_own_z(1)
     gather_3(0)
+    gather_own_x(1)
+    friend_part(1)
     gather_4(0)
     tgt_load.wait()
 
@@ -422,7 +465,7 @@
         values_step(0, s)
 
     gather_1(1)
-    pltpu.make_async_copy(tgt.at[other], tgt.at[other], m_recv.at[2]).wait()
+    tgt_swap.wait_recv()
 
     @pl.loop(0, tiles)
     def _(i):
@@ -437,54 +480,54 @@
     @pl.loop(0, 8)
     def _(s):
         grad_step(0, s)
-
-        @pl.when(s == 3)
-        def _():
-            gather_3(1)
-
-    def scatter_begin(j):
-        scatter_far(j)
-        scatter_q(j, 0)
-        scatter_q(j, 1)
-        scatter_up(j)
-        scatter_q(j, 2)
-        scatter_down(j)
-        scatter_q(j, 3)
-
-    scatter_begin(0)
+        when(s, 1, lambda: scatter_far(0))
+        when(
+            s,
+            3,
+            lambda: gather_3(1),
+            lambda: scatter_q(0, 0),
+            lambda: scatter_up(0),
+            lambda: scatter_q(0, 1),
+        )
+        when(s, 5, lambda: scatter_q(0, 2), lambda: scatter_down(0))
+        when(s, 7, lambda: scatter_q(0, 3), lambda: friend_part(2))
+
     gather_4(1)
 
     @pl.loop(0, 2 * steps)
     def _(s):
         values_step(1, s)
-
-    relay_p(0)
-    far_q_send(0)
+        when(s, 0, lambda: relay_p(0))
+        when(s, 1, lambda: far_q_send(0))
+        when(s, 3, lambda: near_q_up(0))
 
     @pl.loop(0, 8)
     def _(s):
         grad_step(1, s)
-
-        @pl.when(s == 3)
-        def _():
-            near_q_up(0)
-            near_q_down(0)
-
-    scatter_begin(1)
-    relay_q(0)
-    mate_send(0)
-    friend_swap.wait_recv()
+        when(s, 1, lambda: scatter_far(1))
+        when(s, 2, lambda: mate_send(0), lambda: near_q_down(0))
+        when(s, 3, lambda: scatter_up(1), lambda: scatter_q(1, 0), lambda: scatter_q(1, 1))
+        when(s, 4, lambda: relay_q(0))
+        when(s, 5, lambda: scatter_down(1), lambda: scatter_q(1, 2))
+        when(s, 7, lambda: scatter_q(1, 3), lambda: friend_part(3))
+
     own_w_load.wait()
     anchor_load.wait()
     momentum_load.wait()
+    if mask != 1:
+        for i in range(FRIEND_PARTS):
+            friend_swap(i).wait_recv()
     relay_p(1)
+    finish(0)
     far_q_send(1)
-    finish(0)
     near_q_up(1)
+    mate_send(1)
     near_q_down(1)
+    relay_q(1)
+    if mask == 1:
+        for i in range(FRIEND_PARTS):
+            friend_swap(i).wait_recv()
     update_own(0)
-    mate_send(1)
-    relay_q(1)
     update_other(0)
     finish(1)
     update_own(1)
@@ -493,7 +536,8 @@
     for j in range(CHUNKS):
         w_swap(j).wait_send()
     tgt_swap.wait_send()
-    friend_swap.wait_send()
+    for i in range(FRIEND_PARTS):
+        friend_swap(i).wait_send()
 
     @pl.loop(0, tiles)
     def _(i):
@@ -543,8 +587,8 @@
             dma((CHUNKS, N_RS)),
             dma((rows // TILE,)),
             dma((rows // TILE,)),
-            dma((4,)),
-            dma((4,)),
+            dma((3 + FRIEND_PARTS,)),
+            dma((3 + FRIEND_PARTS,)),
             dma((8 + rows // TILE,)),
         ],
         compiler_params=pltpu.CompilerParams(

time: 101 us -> 91.6 us (0.907); the launches traced: 99.8 us -> 91.4 us
  Pallas kernels: 94.1 us -> 85.7 us
    pallas_call x1, Pallas kernels: 94.1 us -> 85.7 us  [run(): pl.pallas_call(functools.partial(kernel, mask, p_rows), out_shape=(jax.Sh...]
where the time goes in v2:
time: 91.6 us; the launch traced here: 91.4 us
  Pallas kernels  85.7 us (94%)
  local copies, waits for them, and re-layouts  3.69 us (4%)
  between operations  1.31 us (1%)
    pallas_call x1, Pallas kernels, run(): pl.pallas_call(functools.partial(kernel, mask, p_rows), out_shape=(jax.Sh...  85.7 us
    unnamed x4, local copies, waits for them, and re-layouts  3.69 us

profile of v2, /device:TPU:1, one launch (start us, length us, event | category | flops | bytes accessed | tf_op | source)
XLA Modules:
  0.0 91.4 jit_solution(14472479746612280075)
XLA Ops:
  1.3 86.4 %conditional.1 = ((f32[320,1024]{1,0:T(8,128)}, f32[320,1024]{1,0:T(8,128)})) conditional(s32[]{:T(128)} %clamp.3, (bf16[1024,5120]{1,0:T(8,128)(2,1)}, bf16[1024,1024]{1,0:T(8,128)(2,1)}, f32[1,5120]{1,0:T(1,128)}, bf16[320,1024]{1,0:T(8,128)(2,1)}, bf16[320,1024]{1,0:T(8,128)(2,1)}, /*index=5*/f32[320,1024]{1,0:T(8,128)}, ...), branch_computations={%region_0.1_spmd, %region_1.2_spmd, %region_2.3_spmd} | conditional | bytes 8 | solution.py:609
  1.7 85.7 %branch_2_fun.1 = (f32[320,1024]{1,0:T(8,128)}, f32[320,1024]{1,0:T(8,128)}) custom-call(bf16[1024,5120]{1,0:T(8,128)(2,1)} %get-tuple-element.68.tokens, bf16[1024,1024]{1,0:T(8,128)(2,1)} %get-tuple-element.69.target, f32[1,5120]{1,0:T(1,128)} %get-tuple-element.70.gain, bf16[320,1024]{1,0:T(8,128)(2,1)} %get-tuple-element.71.weights, ...), custom_call_target="tpu_custom_call" | custom-call | tf_op jit(solution)/shard_map/cond/branch_2_fun/pallas_call | solution.py:558
  87.7 0.0 copy-start
  87.7 2.6 %copy.19 = f32[1,320,1024]{2,1,0:T(8,128)} copy(f32[1,320,1024]{2,1,0:T(8,128)} %bitcast.27) | data formatting | bytes 2621440
  90.4 0.0 copy-done
  90.4 1.1 %copy.20 = f32[1,320,1024]{2,1,0:T(8,128)} copy(f32[1,320,1024]{2,1,0:T(8,128)S(1)} %bitcast.28) | data formatting | bytes 2621440
Async XLA Ops:
  87.7 2.6 %copy-start = (f32[320,1024]{1,0:T(8,128)S(1)}, f32[320,1024]{1,0:T(8,128)}, u32[]{:S(2)}) copy-start(f32[320,1024]{1,0:T(8,128)} %get-tuple-element.80) | copy-start | bytes 3932164

commit v3 on v2

--- a/solution.py
+++ b/solution.py
@@ -23,7 +23,7 @@
 FRIEND_PARTS = 4
 TILE = 128
 STEP = 512
-N_AG = 18
+N_AG = 20
 N_RS = 26
 
 
@@ -85,7 +85,6 @@
     q_rows = BLOCK - p_rows
     PA, PB = (0, half), (BLOCK - half, half)
     QA, QB, Q = (half, q_rows // 2), (ROWS, q_rows // 2), (half, q_rows)
-    H0, H1, ALL = (0, ROWS), (ROWS, ROWS), (0, BLOCK)
 
     def remote(src, dst, send, recv, device):
         return pltpu.make_async_remote_copy(
@@ -99,6 +98,11 @@
 
     sent = []
 
+    barrier = pltpu.get_barrier_semaphore()
+    everyone = (up, up_other, down, down_other, mate, mate_other, sibling, friend)
+    for device in everyone:
+        pl.semaphore_signal(barrier, inc=1, device_id=device, device_id_type=MESH)
+
     def load(src, dst, i):
         copy = pltpu.make_async_copy(src, dst, local.at[i])
         copy.start()
@@ -139,10 +143,6 @@
     anchor_load = load(anchor, anchor_v, 5)
     momentum_load = load(momentum, momentum_v, 6)
 
-    barrier = pltpu.get_barrier_semaphore()
-    everyone = (up, up_other, down, down_other, mate, mate_other, sibling, friend)
-    for device in everyone:
-        pl.semaphore_signal(barrier, inc=1, device_id=device, device_id_type=MESH)
     pl.semaphore_wait(barrier, len(everyone))
 
     def w_swap(j):
@@ -174,7 +174,7 @@
 
     def ag_start(j, i, zz, xx, part, device):
         ag_copy(j, i, zz, xx, part, device).start()
-        sent.append(lambda: ag_copy(j, i, zz, xx, part, device))
+        sent.append(lambda: ag_copy(j, i, z, x, (0, part[1]), mate))
 
     def ag_wait(j, i, zz, xx, part):
         ag_copy(j, i, zz, xx, part, mate).wait_recv()
@@ -190,62 +190,75 @@
             device,
         )
 
-    def own_start(j, i, same, cross):
-        for c, device in ((core, same), (other, cross)):
+    def own_start(j, i, *targets):
+        for c, device in targets:
             own_copy(j, i, c, device).start()
             sent.append(lambda c=c, device=device: own_copy(j, i, c, device))
 
     def own_wait(j, i, zz, xx, h):
-        where = piece(j, zz, xx, (H0, H1)[h])
+        where = piece(j, zz, xx, half_of(h))
         remote(where, where, ag_send.at[j, i], ag_recv.at[j, i + h], mate).wait_recv()
 
+    def p_of(h):
+        return (h * (BLOCK - half), half)
+
+    def q_of(h):
+        return (half + h * (q_rows // 2), q_rows // 2)
+
+    def half_of(h):
+        return (h * ROWS, ROWS)
+
     def gather_own_z(j):
-        own_start(j, 2, up, up_other)
-        own_start(j, 4, down, down_other)
+        own_start(j, 2, (core, up), (other, up_other))
+        own_start(j, 4, (other, down_other), (core, down))
 
     def gather_own_x(j):
-        own_start(j, 0, mate, mate_other)
+        own_start(j, 0, (core, mate), (other, mate_other))
         w_swap(j).start()
 
     def gather_1(j):
-        own_wait(j, 0, z, xm, 0)
-        ag_start(j, 6, z, xm, PA, up)
-        ag_start(j, 8, z, xm, PA, down)
-        own_wait(j, 0, z, xm, 1)
-        ag_start(j, 9, z, xm, PB, down)
-        ag_start(j, 7, z, xm, PB, up)
-        own_wait(j, 2, z_down, x, 0)
-        ag_start(j, 10, z_down, x, H0, up)
-        own_wait(j, 4, z_up, x, 1)
-        ag_start(j, 12, z_up, x, H1, down)
-        own_wait(j, 2, z_down, x, 1)
-        ag_start(j, 11, z_down, x, Q, mate)
-        own_wait(j, 4, z_up, x, 0)
-        ag_start(j, 13, z_up, x, Q, mate)
+        own_wait(j, 2, z_down, x, core)
+        ag_start(j, 10, z_down, x, half_of(core), up)
+        ag_start(j, 12, z_down, x, q_of(core), mate)
+        own_wait(j, 4, z_up, x, other)
+        ag_start(j, 11, z_up, x, half_of(other), down)
+        ag_start(j, 15, z_up, x, q_of(other), mate)
+        own_wait(j, 0, z, xm, core)
+        ag_start(j, 6, z, xm, p_of(core), up)
+        own_wait(j, 0, z, xm, other)
+        ag_start(j, 9, z, xm, p_of(other), down)
+        ag_start(j, 8, z, xm, p_of(other), up)
+        ag_start(j, 7, z, xm, p_of(core), down)
+        own_wait(j, 2, z_down, x, other)
+        ag_start(j, 13, z_down, x, q_of(other), mate)
+        own_wait(j, 4, z_up, x, core)
+        ag_start(j, 14, z_up, x, q_of(core), mate)
 
     def gather_2(j):
-        ag_wait(j, 6, z_down, xm, PA)
-        ag_start(j, 14, z_down, xm, PA, up)
-        ag_wait(j, 9, z_up, xm, PB)
-        ag_start(j, 15, z_up, xm, PB, down)
+        ag_wait(j, 10, z_far, x, half_of(core))
+        ag_start(j, 16, z_far, x, q_of(core), mate)
+        ag_wait(j, 11, z_far, x, half_of(other))
+        ag_start(j, 17, z_far, x, q_of(other), mate)
 
     def gather_3(j):
-        ag_wait(j, 10, z_far, x, H0)
-        ag_start(j, 16, z_far, x, QA, mate)
-        ag_wait(j, 12, z_far, x, H1)
-        ag_start(j, 17, z_far, x, QB, mate)
+        ag_wait(j, 6, z_down, xm, p_of(core))
+        ag_start(j, 18, z_down, xm, p_of(core), up)
+        ag_wait(j, 9, z_up, xm, p_of(other))
+        ag_start(j, 19, z_up, xm, p_of(other), down)
 
     def gather_4(j):
         w_loads[j].wait()
         w_swap(j).wait_recv()
-        ag_wait(j, 7, z_down, xm, PB)
-        ag_wait(j, 8, z_up, xm, PA)
-        ag_wait(j, 11, z_down, xm, Q)
-        ag_wait(j, 13, z_up, xm, Q)
-        ag_wait(j, 14, z_far, xm, PA)
-        ag_wait(j, 15, z_far, xm, PB)
-        ag_wait(j, 16, z_far, xm, QA)
-        ag_wait(j, 17, z_far, xm, QB)
+        ag_wait(j, 7, z_up, xm, p_of(core))
+        ag_wait(j, 8, z_down, xm, p_of(other))
+        ag_wait(j, 12, z_down, xm, q_of(core))
+        ag_wait(j, 13, z_down, xm, q_of(other))
+        ag_wait(j, 14, z_up, xm, q_of(core))
+        ag_wait(j, 15, z_up, xm, q_of(other))
+        ag_wait(j, 16, z_far, xm, q_of(core))
+        ag_wait(j, 17, z_far, xm, q_of(other))
+        ag_wait(j, 18, z_far, xm, p_of(core))
+        ag_wait(j, 19, z_far, xm, p_of(other))
 
     def tile_copy(c, i):
         where = normed.at[tile_of(c, i)]
@@ -386,33 +399,35 @@
         terms = [near_at(j, 0, mate_pb), near_at(j, 1, mate_pb)]
         add_and_send(j, 6, PB, terms, 23, mate_p.at[j, 1], mate)
 
-    def finish(j):
-        def put(part, terms):
-            where = pl.ds(*part)
-            value = grad[j, 7, where, :]
-            for term in terms:
-                value = value + term[...].astype(F32)
-            total[j, where, :] = value
-
+    def most_of_total(j):
         rs_wait(j, 3, from_mate.at[j, 3])
-        rs_wait(j, 13, near_at(j, 0, PA))
-        rs_wait(j, 11, near_at(j, 1, PA))
+        for i, d, part in (
+            (13, 0, PA),
+            (11, 1, PA),
+            (9, 0, PB),
+            (15, 1, PB),
+            (20, 0, QA),
+            (19, 1, QA),
+            (18, 0, QB),
+            (21, 1, QB),
+        ):
+            rs_wait(j, i, near_at(j, d, part))
+        value = grad[j, 7] + near[j, 0, :BLOCK, :].astype(F32)
+        total[j] = value + near[j, 1, :BLOCK, :].astype(F32)
+        total[j, half : half + q_rows, :] += from_mate[j, 3].astype(F32)
+
+    def rest_of_total(j):
         rs_wait(j, 22, mate_p.at[j, 0])
-        put(PA, [near_at(j, 0, PA), near_at(j, 1, PA), mate_p.at[j, 0]])
-        rs_wait(j, 9, near_at(j, 0, PB))
-        rs_wait(j, 15, near_at(j, 1, PB))
         rs_wait(j, 23, mate_p.at[j, 1])
-        put(PB, [near_at(j, 0, PB), near_at(j, 1, PB), mate_p.at[j, 1]])
-        rs_wait(j, 20, near_at(j, 0, QA))
-        rs_wait(j, 19, near_at(j, 1, QA))
-        put(QA, [near_at(j, 0, QA), near_at(j, 1, QA), mate_q(j, 3, True)])
-        rs_wait(j, 18, near_at(j, 0, QB))
-        rs_wait(j, 21, near_at(j, 1, QB))
-        put(QB, [near_at(j, 0, QB), near_at(j, 1, QB), mate_q(j, 3, False)])
-        theirs = pl.ds(pl.multiple_of(other * ROWS, 64), ROWS)
-        rs_start(j, 24, total.at[j, theirs], swapped.at[j], sibling)
-
-    def update(columns, gradient):
+        for h in (other, core):
+            where = pl.ds(pl.multiple_of(h * (BLOCK - half), 16), half)
+            total[j, where, :] += mate_p[j, h].astype(F32)
+            if h is other:
+                theirs = pl.ds(pl.multiple_of(other * ROWS, 64), ROWS)
+                rs_start(j, 24, total.at[j, theirs], swapped.at[j], sibling)
+
+    def update(c, j, gradient):
+        columns = cols(c, j)
         fast = own_w[:, columns].astype(F32) - INNER_RATE * (gradient * scale)
         mixed = 0.5 * fast + 0.5 * partner[:, columns].astype(F32)
         base = anchor_v[:, columns]
@@ -422,11 +437,16 @@
 
     def update_own(j):
         mine = pl.ds(pl.multiple_of(core * ROWS, 64), ROWS)
-        update(cols(core, j), total[j, mine, :])
+        update(core, j, total[j, mine, :])
 
     def update_other(j):
         rs_wait(j, 24, swapped.at[j])
-        update(cols(other, j), swapped[j])
+        update(other, j, swapped[j])
+
+    def drain():
+        for copy in sent:
+            copy().wait_send()
+        sent.clear()
 
     def when(s, step, *todo):
         @pl.when(s == step)
@@ -453,10 +473,10 @@
 
     gather_1(0)
     gather_2(0)
-    gather_own_z(1)
-    gather_3(0)
     gather_own_x(1)
     friend_part(1)
+    gather_3(0)
+    gather_own_z(1)
     gather_4(0)
     tgt_load.wait()
 
@@ -518,7 +538,8 @@
         for i in range(FRIEND_PARTS):
             friend_swap(i).wait_recv()
     relay_p(1)
-    finish(0)
+    most_of_total(0)
+    rest_of_total(0)
     far_q_send(1)
     near_q_up(1)
     mate_send(1)
@@ -529,9 +550,7 @@
             friend_swap(i).wait_recv()
     update_own(0)
     update_other(0)
-    finish(1)
-    update_own(1)
-    update_other(1)
+    most_of_total(1)
 
     for j in range(CHUNKS):
         w_swap(j).wait_send()
@@ -543,26 +562,25 @@
     def _(i):
         tile_copy(core, i).wait_send()
 
-    for copy in sent:
-        copy().wait_send()
+    drain()
+    rest_of_total(1)
+    update_own(1)
+    update_other(1)
+    drain()
 
 
 def run(mask, p_rows, collective_id, tokens, target, gain, weights, previous, anchor, momentum):
     rows, width = tokens.shape
     kv = target.shape[1]
     half, q_rows = p_rows // 2, BLOCK - p_rows
-    anywhere = pl.BlockSpec(memory_space=pl.ANY)
-    here = pl.BlockSpec(memory_space=pltpu.VMEM)
+    anywhere = pl.BlockSpec(memory_space=pltpu.HBM)
     vmem, dma = pltpu.VMEM, pltpu.SemaphoreType.DMA
     side = CHUNKS * CHUNK
     return pl.pallas_call(
         functools.partial(kernel, mask, p_rows),
-        out_shape=(
-            jax.ShapeDtypeStruct((ROWS, kv), F32),
-            jax.ShapeDtypeStruct((ROWS, kv), F32),
-        ),
+        out_shape=(jax.ShapeDtypeStruct((ROWS, kv), F32),) * 2,
         in_specs=[anywhere] * 7,
-        out_specs=(here, here),
+        out_specs=(pl.BlockSpec(memory_space=pltpu.VMEM),) * 2,
         scratch_shapes=[
             vmem((2 * rows, width), BF16),
             vmem((CHUNKS, width, CHUNK), BF16),
@@ -594,7 +612,7 @@
         compiler_params=pltpu.CompilerParams(
             collective_id=collective_id,
             has_side_effects=True,
-            vmem_limit_bytes=63 << 20,
+            vmem_limit_bytes=56 << 20,
         ),
     )(tokens, target, gain, weights, previous, anchor, momentum)
 

time: 91.6 us -> 84.6 us (0.924)
  Pallas kernels: 85.7 us -> 80.3 us
  local copies, waits for them, and re-layouts: 3.69 us -> 2.11 us
    pallas_call x1, Pallas kernels: 85.7 us -> 80.3 us  [run(): pl.pallas_call(functools.partial(kernel, mask, p_rows), out_shape=(jax.Sh...]
    unnamed x4 -> x2, local copies, waits for them, and re-layouts: 3.69 us -> 2.11 us
where the time goes in v3:
time: 84.6 us; the launch traced here: 84.4 us
  Pallas kernels  80.3 us (95%)
  local copies, waits for them, and re-layouts  2.11 us (2%)
  between operations  1.3 us (2%)
    pallas_call x1, Pallas kernels, run(): pl.pallas_call(functools.partial(kernel, mask, p_rows), out_shape=(jax.Sh...  80.3 us
    unnamed x2, local copies, waits for them, and re-layouts  2.11 us

profile of v3, /device:TPU:1, one launch (start us, length us, event | category | flops | bytes accessed | tf_op | source)
XLA Modules:
  0.0 84.4 jit_solution(1009308471713261421)
XLA Ops:
  1.3 81.0 %conditional.1 = ((f32[320,1024]{1,0:T(8,128)S(1)}, f32[320,1024]{1,0:T(8,128)S(1)})) conditional(s32[]{:T(128)} %clamp.3, (bf16[1024,5120]{1,0:T(8,128)(2,1)}, bf16[1024,1024]{1,0:T(8,128)(2,1)}, f32[1,5120]{1,0:T(1,128)}, bf16[320,1024]{1,0:T(8,128)(2,1)}, bf16[320,1024]{1,0:T(8,128)(2,1)}, /*index=5*/f32[320,1024]{1,0:T(8,128)}, ...), branch_computations={%region_0.1_spmd, %region_1.2_spmd, %region_2.3_spmd} | conditional | bytes 8 | solution.py:627
  1.5 80.3 %branch_1_fun.1 = (f32[320,1024]{1,0:T(8,128)S(1)}, f32[320,1024]{1,0:T(8,128)S(1)}) custom-call(bf16[1024,5120]{1,0:T(8,128)(2,1)} %get-tuple-element.59.tokens, bf16[1024,1024]{1,0:T(8,128)(2,1)} %get-tuple-element.60.target, f32[1,5120]{1,0:T(1,128)} %get-tuple-element.61.gain, bf16[320,1024]{1,0:T(8,128)(2,1)} %get-tuple-element.62.weights, ...), custom_call_target="tpu_custom_call" | custom-call | tf_op jit(solution)/shard_map/cond/branch_1_fun/pallas_call | solution.py:579
  82.3 1.1 %copy.19 = f32[1,320,1024]{2,1,0:T(8,128)} copy(f32[1,320,1024]{2,1,0:T(8,128)S(1)} %bitcast.27) | data formatting | bytes 2621440
  83.4 1.1 %copy.20 = f32[1,320,1024]{2,1,0:T(8,128)} copy(f32[1,320,1024]{2,1,0:T(8,128)S(1)} %bitcast.28) | data formatting | bytes 2621440

commit v4 on v3

--- a/solution.py
+++ b/solution.py
@@ -21,6 +21,8 @@
 CHUNK = 256
 CHUNKS = 2
 FRIEND_PARTS = 4
+SPLIT = (352, 352)
+SPLIT_X = (416, 416)
 TILE = 128
 STEP = 512
 N_AG = 20
@@ -29,6 +31,7 @@
 
 def kernel(
     mask,
+    p_gather,
     p_rows,
     tokens,
     target,
@@ -48,9 +51,10 @@
     from_mate,
     far,
     near,
-    mate_p,
+    last,
+    last_mate,
     total,
-    swapped,
+    sibling_own,
     own_w,
     partner,
     anchor_v,
@@ -60,6 +64,7 @@
     ag_recv,
     rs_send,
     rs_recv,
+    last_recv,
     n_send,
     n_recv,
     m_send,
@@ -76,6 +81,9 @@
     up, up_other = [(rep, z_up * 4 + x * 2 + c) for c in (core, other)]
     down, down_other = [(rep, z_down * 4 + x * 2 + c) for c in (core, other)]
     mate, mate_other = [(rep, z * 4 + (1 - x) * 2 + c) for c in (core, other)]
+    up_core = [(rep, z_up * 4 + x * 2 + c) for c in range(2)]
+    down_core = [(rep, z_down * 4 + x * 2 + c) for c in range(2)]
+    mate_core = [(rep, z * 4 + (1 - x) * 2 + c) for c in range(2)]
     sibling = (rep, z * 4 + x * 2 + other)
     friend = (rep + mask - 2 * mask * lax.rem(rep // mask, 2), at)
 
@@ -199,11 +207,14 @@
         where = piece(j, zz, xx, half_of(h))
         remote(where, where, ag_send.at[j, i], ag_recv.at[j, i + h], mate).wait_recv()
 
+    p_half = p_gather // 2
+    q_half = ROWS - p_half
+
     def p_of(h):
-        return (h * (BLOCK - half), half)
+        return (h * (BLOCK - p_half), p_half)
 
     def q_of(h):
-        return (half + h * (q_rows // 2), q_rows // 2)
+        return (p_half + h * q_half, q_half)
 
     def half_of(h):
         return (h * ROWS, ROWS)
@@ -225,6 +236,8 @@
         ag_start(j, 15, z_up, x, q_of(other), mate)
         own_wait(j, 0, z, xm, core)
         ag_start(j, 6, z, xm, p_of(core), up)
+
+    def gather_1_rest(j):
         own_wait(j, 0, z, xm, other)
         ag_start(j, 9, z, xm, p_of(other), down)
         ag_start(j, 8, z, xm, p_of(other), up)
@@ -305,15 +318,36 @@
     def rs_copy(j, i, src, dst, device):
         return remote(src, dst, rs_send.at[j, i], rs_recv.at[j, i], device)
 
+    def rs_sent(j, i, src):
+        whole, count = src.dtype == F32, src.shape[0]
+
+        def again():
+            where = sibling_own.at[j] if whole else grad_half.at[j, 0, pl.ds(0, count)]
+            return rs_copy(j, i, where, where, mate)
+
+        sent.append(again)
+
     def rs_start(j, i, src, dst, device):
         rs_copy(j, i, src, dst, device).start()
-        is_total, count = src.dtype == F32, src.shape[0]
-
-        def again():
-            where = (total if is_total else grad_half.at[j]).at[0, pl.ds(0, count)]
-            return rs_copy(j, i, where, where, mate)
-
-        sent.append(again)
+        rs_sent(j, i, src)
+
+    P_LAST, Q_LAST = pl.ds(0, half), pl.ds(half, q_rows // 2)
+
+    def last_at(j, c, kind):
+        rows = Q_LAST if kind % 2 else P_LAST
+        return last_mate.at[j, c, rows] if kind > 3 else last.at[j, c, kind // 2, rows]
+
+    def last_start(j, i, src, kind, h):
+        device = (up_core, down_core, mate_core)[kind // 2][h]
+        copy = remote(
+            src, last_at(j, core, kind), rs_send.at[j, i], last_recv.at[j, core, kind], device
+        )
+        copy.start()
+        rs_sent(j, i, src)
+
+    def last_wait(j, c, kind):
+        where = last_at(j, c, kind)
+        remote(where, where, rs_send.at[j, 0], last_recv.at[j, c, kind], mate).wait_recv()
 
     def rs_wait(j, i, dst):
         rs_copy(j, i, dst, dst, mate).wait_recv()
@@ -323,7 +357,7 @@
 
     far_p = ((0, half), (half, half))
     far_q = (2 * half, q_rows // 2)
-    mate_pa, mate_pb = (BLOCK, half), (BLOCK + half, half)
+    mate_pa, mate_pb = (0, half), (half, half)
 
     def near_at(j, d, part):
         return near.at[j, d, pl.ds(*part)]
@@ -332,7 +366,11 @@
         return far.at[j, d, pl.ds(*part)]
 
     def scatter_q(j, i):
-        rs_start(j, i, out_of(j, 2 * i, Q), from_mate.at[j, i], mate)
+        if i < 3:
+            rs_start(j, i, out_of(j, 2 * i, Q), from_mate.at[j, i], mate)
+        else:
+            last_start(j, 3, out_of(j, 6, QA), 5, 0)
+            last_start(j, 25, out_of(j, 6, QB), 5, 1)
 
     def scatter_far(j):
         for c in range(2):
@@ -341,28 +379,33 @@
 
     def scatter_up(j):
         rs_start(j, 8, out_of(j, 2, PB), near_at(j, 0, mate_pb), up)
-        rs_start(j, 9, out_of(j, 3, PB), near_at(j, 0, PB), up)
+        last_start(j, 9, out_of(j, 3, PB), 0, 1)
 
     def scatter_down(j):
         rs_start(j, 10, out_of(j, 4, PA), near_at(j, 1, mate_pa), down)
-        rs_start(j, 11, out_of(j, 5, PA), near_at(j, 1, PA), down)
-
-    def add_and_send(j, s, part, terms, i, dst, device):
+        last_start(j, 11, out_of(j, 5, PA), 2, 0)
+
+    def scatter_own(j):
+        theirs = pl.ds(pl.multiple_of(other * ROWS, 64), ROWS)
+        rs_start(j, 24, grad.at[j, 7, theirs], sibling_own.at[j], sibling)
+
+    def added(j, s, part, terms):
         where = pl.ds(*part)
         value = grad[j, s, where, :]
         for term in terms:
             value = value + term[...].astype(F32)
         grad_half[j, s, where, :] = value.astype(BF16)
-        rs_start(j, i, out_of(j, s, part), dst, device)
+        return out_of(j, s, part)
 
     def relay_p(j):
-        for c in range(2):
-            rs_wait(j, 4 + c, far_at(j, 0, far_p[c]))
-            dst = near_at(j, 0, PA if c else mate_pa)
-            add_and_send(j, 2 + c, PA, [far_at(j, 0, far_p[c])], 12 + c, dst, up)
-            rs_wait(j, 6 + c, far_at(j, 1, far_p[c]))
-            dst = near_at(j, 1, PB if c else mate_pb)
-            add_and_send(j, 4 + c, PB, [far_at(j, 1, far_p[c])], 14 + c, dst, down)
+        rs_wait(j, 4, far_at(j, 0, far_p[0]))
+        rs_start(j, 12, added(j, 2, PA, [far_at(j, 0, far_p[0])]), near_at(j, 0, mate_pa), up)
+        rs_wait(j, 6, far_at(j, 1, far_p[0]))
+        rs_start(j, 14, added(j, 4, PB, [far_at(j, 1, far_p[0])]), near_at(j, 1, mate_pb), down)
+        rs_wait(j, 5, far_at(j, 0, far_p[1]))
+        last_start(j, 13, added(j, 3, PA, [far_at(j, 0, far_p[1])]), 0, 0)
+        rs_wait(j, 7, far_at(j, 1, far_p[1]))
+        last_start(j, 15, added(j, 5, PB, [far_at(j, 1, far_p[1])]), 2, 1)
 
     def mate_q(j, i, lower):
         start, count = (0, q_rows // 2) if lower else (q_rows // 2, q_rows // 2)
@@ -370,61 +413,60 @@
 
     def far_q_send(j):
         rs_wait(j, 0, from_mate.at[j, 0])
-        add_and_send(j, 1, QA, [mate_q(j, 0, True)], 16, far_at(j, 0, far_q), up)
-        add_and_send(j, 1, QB, [mate_q(j, 0, False)], 17, far_at(j, 1, far_q), down)
+        rs_start(j, 16, added(j, 1, QA, [mate_q(j, 0, True)]), far_at(j, 0, far_q), up)
+        rs_start(j, 17, added(j, 1, QB, [mate_q(j, 0, False)]), far_at(j, 1, far_q), down)
 
     def near_q_up(j):
         rs_wait(j, 1, from_mate.at[j, 1])
-        add_and_send(j, 3, QB, [mate_q(j, 1, False)], 18, near_at(j, 0, QB), up)
+        last_start(j, 18, added(j, 3, QB, [mate_q(j, 1, False)]), 1, 1)
 
     def near_q_down(j):
         rs_wait(j, 2, from_mate.at[j, 2])
-        add_and_send(j, 5, QA, [mate_q(j, 2, True)], 19, near_at(j, 1, QA), down)
+        last_start(j, 19, added(j, 5, QA, [mate_q(j, 2, True)]), 3, 0)
 
     def relay_q(j):
         rs_wait(j, 16, far_at(j, 0, far_q))
         terms = [mate_q(j, 1, True), far_at(j, 0, far_q)]
-        add_and_send(j, 3, QA, terms, 20, near_at(j, 0, QA), up)
+        last_start(j, 20, added(j, 3, QA, terms), 1, 0)
         rs_wait(j, 17, far_at(j, 1, far_q))
         terms = [mate_q(j, 2, False), far_at(j, 1, far_q)]
-        add_and_send(j, 5, QB, terms, 21, near_at(j, 1, QB), down)
+        last_start(j, 21, added(j, 5, QB, terms), 3, 1)
 
     def mate_send(j):
         rs_wait(j, 12, near_at(j, 0, mate_pa))
         rs_wait(j, 10, near_at(j, 1, mate_pa))
         terms = [near_at(j, 0, mate_pa), near_at(j, 1, mate_pa)]
-        add_and_send(j, 6, PA, terms, 22, mate_p.at[j, 0], mate)
+        last_start(j, 22, added(j, 6, PA, terms), 4, 0)
         rs_wait(j, 8, near_at(j, 0, mate_pb))
         rs_wait(j, 14, near_at(j, 1, mate_pb))
         terms = [near_at(j, 0, mate_pb), near_at(j, 1, mate_pb)]
-        add_and_send(j, 6, PB, terms, 23, mate_p.at[j, 1], mate)
+        last_start(j, 23, added(j, 6, PB, terms), 4, 1)
+
+    p_start, q_start = core * (q_rows // 2), other * half
 
     def most_of_total(j):
-        rs_wait(j, 3, from_mate.at[j, 3])
-        for i, d, part in (
-            (13, 0, PA),
-            (11, 1, PA),
-            (9, 0, PB),
-            (15, 1, PB),
-            (20, 0, QA),
-            (19, 1, QA),
-            (18, 0, QB),
-            (21, 1, QB),
-        ):
-            rs_wait(j, i, near_at(j, d, part))
-        value = grad[j, 7] + near[j, 0, :BLOCK, :].astype(F32)
-        total[j] = value + near[j, 1, :BLOCK, :].astype(F32)
-        total[j, half : half + q_rows, :] += from_mate[j, 3].astype(F32)
+        rs_wait(j, 24, sibling_own.at[j])
+        for k, c in enumerate((core, other)):
+            for kind in (0, 2, 1, 3, 5):
+                last_wait(j, c, kind)
+            for start, rows, part in ((p_start, P_LAST, half), (q_start, Q_LAST, q_rows // 2)):
+                here = pl.ds(pl.multiple_of(start, 16), part)
+                if k:
+                    value = sibling_own[j, here, :]
+                else:
+                    value = grad[j, 7, pl.ds(pl.multiple_of(core * ROWS + start, 16), part), :]
+                value = value + last[j, c, 0, rows, :].astype(F32)
+                value = value + last[j, c, 1, rows, :].astype(F32)
+                if rows is Q_LAST:
+                    value = value + last_mate[j, c, rows, :].astype(F32)
+                total[j, k, here, :] = value
 
     def rest_of_total(j):
-        rs_wait(j, 22, mate_p.at[j, 0])
-        rs_wait(j, 23, mate_p.at[j, 1])
-        for h in (other, core):
-            where = pl.ds(pl.multiple_of(h * (BLOCK - half), 16), half)
-            total[j, where, :] += mate_p[j, h].astype(F32)
-            if h is other:
-                theirs = pl.ds(pl.multiple_of(other * ROWS, 64), ROWS)
-                rs_start(j, 24, total.at[j, theirs], swapped.at[j], sibling)
+        for k, c in enumerate((core, other)):
+            last_wait(j, c, 4)
+            here = pl.ds(pl.multiple_of(p_start, 16), half)
+            total[j, k, here, :] += last_mate[j, c, P_LAST, :].astype(F32)
+            update(c, j, total[j, k])
 
     def update(c, j, gradient):
         columns = cols(c, j)
@@ -435,14 +477,6 @@
         new_momentum[:, columns] = moment
         new_anchor[:, columns] = base - OUTER_RATE * INNER_RATE * moment
 
-    def update_own(j):
-        mine = pl.ds(pl.multiple_of(core * ROWS, 64), ROWS)
-        update(core, j, total[j, mine, :])
-
-    def update_other(j):
-        rs_wait(j, 24, swapped.at[j])
-        update(other, j, swapped[j])
-
     def drain():
         for copy in sent:
             copy().wait_send()
@@ -472,6 +506,7 @@
         norm_tile(i)
 
     gather_1(0)
+    gather_1_rest(0)
     gather_2(0)
     gather_own_x(1)
     friend_part(1)
@@ -483,8 +518,8 @@
     @pl.loop(0, steps)
     def _(s):
         values_step(0, s)
-
-    gather_1(1)
+        when(s, 0, lambda: gather_1(1))
+
     tgt_swap.wait_recv()
 
     @pl.loop(0, tiles)
@@ -494,13 +529,12 @@
     @pl.loop(steps, 2 * steps)
     def _(s):
         values_step(0, s)
-
-    gather_2(1)
+        when(s, steps, lambda: gather_1_rest(1))
 
     @pl.loop(0, 8)
     def _(s):
         grad_step(0, s)
-        when(s, 1, lambda: scatter_far(0))
+        when(s, 1, lambda: gather_2(1), lambda: scatter_far(0))
         when(
             s,
             3,
@@ -510,7 +544,7 @@
             lambda: scatter_q(0, 1),
         )
         when(s, 5, lambda: scatter_q(0, 2), lambda: scatter_down(0))
-        when(s, 7, lambda: scatter_q(0, 3), lambda: friend_part(2))
+        when(s, 7, lambda: scatter_own(0), lambda: scatter_q(0, 3), lambda: friend_part(2))
 
     gather_4(1)
 
@@ -524,12 +558,12 @@
     @pl.loop(0, 8)
     def _(s):
         grad_step(1, s)
-        when(s, 1, lambda: scatter_far(1))
-        when(s, 2, lambda: mate_send(0), lambda: near_q_down(0))
-        when(s, 3, lambda: scatter_up(1), lambda: scatter_q(1, 0), lambda: scatter_q(1, 1))
-        when(s, 4, lambda: relay_q(0))
+        when(s, 0, lambda: near_q_down(0))
+        when(s, 1, lambda: scatter_far(1), lambda: scatter_q(1, 0))
+        when(s, 2, lambda: mate_send(0))
+        when(s, 3, lambda: scatter_up(1), lambda: scatter_q(1, 1), lambda: relay_q(0))
         when(s, 5, lambda: scatter_down(1), lambda: scatter_q(1, 2))
-        when(s, 7, lambda: scatter_q(1, 3), lambda: friend_part(3))
+        when(s, 7, lambda: scatter_own(1), lambda: scatter_q(1, 3), lambda: friend_part(3))
 
     own_w_load.wait()
     anchor_load.wait()
@@ -539,7 +573,6 @@
             friend_swap(i).wait_recv()
     relay_p(1)
     most_of_total(0)
-    rest_of_total(0)
     far_q_send(1)
     near_q_up(1)
     mate_send(1)
@@ -548,8 +581,7 @@
     if mask == 1:
         for i in range(FRIEND_PARTS):
             friend_swap(i).wait_recv()
-    update_own(0)
-    update_other(0)
+    rest_of_total(0)
     most_of_total(1)
 
     for j in range(CHUNKS):
@@ -564,12 +596,9 @@
 
     drain()
     rest_of_total(1)
-    update_own(1)
-    update_other(1)
-    drain()
-
-
-def run(mask, p_rows, collective_id, tokens, target, gain, weights, previous, anchor, momentum):
+
+
+def run(mask, p_gather, p_rows, collective_id, tokens, target, gain, weights, previous, anchor, momentum):
     rows, width = tokens.shape
     kv = target.shape[1]
     half, q_rows = p_rows // 2, BLOCK - p_rows
@@ -577,7 +606,7 @@
     vmem, dma = pltpu.VMEM, pltpu.SemaphoreType.DMA
     side = CHUNKS * CHUNK
     return pl.pallas_call(
-        functools.partial(kernel, mask, p_rows),
+        functools.partial(kernel, mask, p_gather, p_rows),
         out_shape=(jax.ShapeDtypeStruct((ROWS, kv), F32),) * 2,
         in_specs=[anywhere] * 7,
         out_specs=(pl.BlockSpec(memory_space=pltpu.VMEM),) * 2,
@@ -588,11 +617,12 @@
             vmem((CHUNKS, 8, BLOCK, CHUNK), BF16),
             vmem((2, rows, side), BF16),
             vmem((2 * rows, CHUNK), BF16),
-            vmem((CHUNKS, 4, q_rows, CHUNK), BF16),
+            vmem((CHUNKS, 3, q_rows, CHUNK), BF16),
             vmem((CHUNKS, 2, p_rows + q_rows // 2, CHUNK), BF16),
-            vmem((CHUNKS, 2, BLOCK + p_rows, CHUNK), BF16),
-            vmem((CHUNKS, 2, half, CHUNK), BF16),
-            vmem((CHUNKS, BLOCK, CHUNK), F32),
+            vmem((CHUNKS, 2, p_rows, CHUNK), BF16),
+            vmem((CHUNKS, 2, 2, ROWS, CHUNK), BF16),
+            vmem((CHUNKS, 2, ROWS, CHUNK), BF16),
+            vmem((CHUNKS, 2, ROWS, CHUNK), F32),
             vmem((CHUNKS, ROWS, CHUNK), F32),
             vmem((ROWS, kv), BF16),
             vmem((ROWS, kv), BF16),
@@ -603,6 +633,7 @@
             dma((CHUNKS, N_AG)),
             dma((CHUNKS, N_RS)),
             dma((CHUNKS, N_RS)),
+            dma((CHUNKS, 2, 6)),
             dma((rows // TILE,)),
             dma((rows // TILE,)),
             dma((3 + FRIEND_PARTS,)),
@@ -621,7 +652,7 @@
     bit_count = lax.axis_size("rep").bit_length() - 1
     chosen_bit = jnp.remainder(step_bit, jnp.int32(bit_count))
     branches = [
-        functools.partial(run, 2**bit, 416 if bit == 0 else 352, bit)
+        functools.partial(run, 2**bit, *(SPLIT_X if bit == 0 else SPLIT), bit)
         for bit in range(bit_count)
     ]
     moment_new, anchor_new = lax.switch(

time: 84.6 us -> 83 us (0.981)
  Pallas kernels: 80.3 us -> 78.8 us
    pallas_call x1, Pallas kernels: 80.3 us -> 78.8 us  [run(): pl.pallas_call(functools.partial(kernel, mask, p_gather, p_rows), out_sha...]
where the time goes in v4:
time: 83 us; the launch traced here: 82.9 us
  Pallas kernels  78.8 us (95%)
  local copies, waits for them, and re-layouts  2.11 us (3%)
  between operations  1.3 us (2%)
    pallas_call x1, Pallas kernels, run(): pl.pallas_call(functools.partial(kernel, mask, p_gather, p_rows), out_sha...  78.8 us
    unnamed x2, local copies, waits for them, and re-layouts  2.11 us

profile of v4, /device:TPU:1, one launch (start us, length us, event | category | flops | bytes accessed | tf_op | source)
XLA Modules:
  0.0 82.9 jit_solution(12796102317943573)
XLA Ops:
  1.3 79.5 %conditional.1 = ((f32[320,1024]{1,0:T(8,128)S(1)}, f32[320,1024]{1,0:T(8,128)S(1)})) conditional(s32[]{:T(128)} %clamp.3, (bf16[1024,5120]{1,0:T(8,128)(2,1)}, bf16[1024,1024]{1,0:T(8,128)(2,1)}, f32[1,5120]{1,0:T(1,128)}, bf16[320,1024]{1,0:T(8,128)(2,1)}, bf16[320,1024]{1,0:T(8,128)(2,1)}, /*index=5*/f32[320,1024]{1,0:T(8,128)}, ...), branch_computations={%region_0.1_spmd, %region_1.2_spmd, %region_2.3_spmd} | conditional | bytes 8 | solution.py:658
  1.7 78.8 %branch_2_fun.1 = (f32[320,1024]{1,0:T(8,128)S(1)}, f32[320,1024]{1,0:T(8,128)S(1)}) custom-call(bf16[1024,5120]{1,0:T(8,128)(2,1)} %get-tuple-element.68.tokens, bf16[1024,1024]{1,0:T(8,128)(2,1)} %get-tuple-element.69.target, f32[1,5120]{1,0:T(1,128)} %get-tuple-element.70.gain, bf16[320,1024]{1,0:T(8,128)(2,1)} %get-tuple-element.71.weights, ...), custom_call_target="tpu_custom_call" | custom-call | tf_op jit(solution)/shard_map/cond/branch_2_fun/pallas_call | solution.py:608
  80.8 1.1 %copy.19 = f32[1,320,1024]{2,1,0:T(8,128)} copy(f32[1,320,1024]{2,1,0:T(8,128)S(1)} %bitcast.27) | data formatting | bytes 2621440
  81.9 1.1 %copy.20 = f32[1,320,1024]{2,1,0:T(8,128)} copy(f32[1,320,1024]{2,1,0:T(8,128)S(1)} %bitcast.28) | data formatting | bytes 2621440

commit v5 on v4

--- a/solution.py
+++ b/solution.py
@@ -534,12 +534,11 @@
     @pl.loop(0, 8)
     def _(s):
         grad_step(0, s)
-        when(s, 1, lambda: gather_2(1), lambda: scatter_far(0))
+        when(s, 1, lambda: gather_2(1), lambda: scatter_far(0), lambda: scatter_q(0, 0))
         when(
             s,
             3,
             lambda: gather_3(1),
-            lambda: scatter_q(0, 0),
             lambda: scatter_up(0),
             lambda: scatter_q(0, 1),
         )
@@ -572,7 +571,6 @@
         for i in range(FRIEND_PARTS):
             friend_swap(i).wait_recv()
     relay_p(1)
-    most_of_total(0)
     far_q_send(1)
     near_q_up(1)
     mate_send(1)
@@ -581,6 +579,7 @@
     if mask == 1:
         for i in range(FRIEND_PARTS):
             friend_swap(i).wait_recv()
+    most_of_total(0)
     rest_of_total(0)
     most_of_total(1)
 
@@ -648,6 +647,27 @@
     )(tokens, target, gain, weights, previous, anchor, momentum)
 
 
+def hand_over(moment, anchor, moment_out, anchor_out, sems):
+    copies = [
+        pltpu.make_async_copy(moment, moment_out, sems.at[0]),
+        pltpu.make_async_copy(anchor, anchor_out, sems.at[1]),
+    ]
+    for copy in copies:
+        copy.start()
+    for copy in copies:
+        copy.wait()
+
+
+def results(moment, anchor):
+    return pl.pallas_call(
+        hand_over,
+        out_shape=(jax.ShapeDtypeStruct(moment.shape, F32),) * 2,
+        in_specs=[pl.BlockSpec(memory_space=pl.ANY)] * 2,
+        out_specs=(pl.BlockSpec(memory_space=pltpu.HBM),) * 2,
+        scratch_shapes=[pltpu.SemaphoreType.DMA((2,))],
+    )(moment, anchor)
+
+
 def shards(step_bit, tokens, target, norm_gain, weights, previous, anchor, momentum):
     bit_count = lax.axis_size("rep").bit_length() - 1
     chosen_bit = jnp.remainder(step_bit, jnp.int32(bit_count))
@@ -666,6 +686,7 @@
         anchor[0],
         momentum[0],
     )
+    moment_new, anchor_new = results(moment_new, anchor_new)
     return (moment_new[None], anchor_new[None])
 
 

time: 83 us -> 81.1 us (0.977)
  local copies, waits for them, and re-layouts: 2.11 us -> 0 us
    unnamed x2 -> x0, local copies, waits for them, and re-layouts: 2.11 us -> none
    pallas_call x1, Pallas kernels: 78.8 us -> 77.3 us  [run(): pl.pallas_call(functools.partial(kernel, mask, p_gather, p_rows), out_sha...]
    pallas_call x0 -> x1, Pallas kernels: none -> 1.51 us  [results(): pl.pallas_call(hand_over, out_shape=(jax.ShapeDtypeStruct(moment.shape, F...]
where the time goes in v5:
time: 81.1 us; the launch traced here: 81 us
  Pallas kernels  78.8 us (97%)
  between operations  1.5 us (2%)
    pallas_call x1, Pallas kernels, run(): pl.pallas_call(functools.partial(kernel, mask, p_gather, p_rows), out_sha...  77.3 us

profile of v5, /device:TPU:1, one launch (start us, length us, event | category | flops | bytes accessed | tf_op | source)
XLA Modules:
  0.0 81.0 jit_solution(3983965080105372223)
XLA Ops:
  1.3 78.0 %conditional.1 = ((f32[320,1024]{1,0:T(8,128)S(1)}, f32[320,1024]{1,0:T(8,128)S(1)})) conditional(s32[]{:T(128)} %clamp.3, (bf16[1024,5120]{1,0:T(8,128)(2,1)}, bf16[1024,1024]{1,0:T(8,128)(2,1)}, f32[1,5120]{1,0:T(1,128)}, bf16[320,1024]{1,0:T(8,128)(2,1)}, bf16[320,1024]{1,0:T(8,128)(2,1)}, /*index=5*/f32[320,1024]{1,0:T(8,128)}, ...), branch_computations={%region_0.1_spmd, %region_1.2_spmd, %region_2.3_spmd} | conditional | bytes 8 | solution.py:678
  1.5 77.3 %branch_1_fun.1 = (f32[320,1024]{1,0:T(8,128)S(1)}, f32[320,1024]{1,0:T(8,128)S(1)}) custom-call(bf16[1024,5120]{1,0:T(8,128)(2,1)} %get-tuple-element.49.tokens, bf16[1024,1024]{1,0:T(8,128)(2,1)} %get-tuple-element.50.target, f32[1,5120]{1,0:T(1,128)} %get-tuple-element.51.gain, bf16[320,1024]{1,0:T(8,128)(2,1)} %get-tuple-element.52.weights, ...), custom_call_target="tpu_custom_call" | custom-call | tf_op jit(solution)/shard_map/cond/branch_1_fun/pallas_call | solution.py:607
  79.3 1.5 %shard_map.95 = (f32[320,1024]{1,0:T(8,128)}, f32[320,1024]{1,0:T(8,128)}) custom-call(f32[320,1024]{1,0:T(8,128)S(1)} %get-tuple-element.69.moment, f32[320,1024]{1,0:T(8,128)S(1)} %get-tuple-element.70.anchor), custom_call_target="tpu_custom_call" | custom-call | tf_op jit(solution)/shard_map/pallas_call | solution.py:662
